TPU v7x, 128 devices: a whole 4x4x4 slice. The times are simulated.
128 devices in a mesh: pair: 2 (over z_hi), row: 32 (over x, y, core), col: 2 (over z_lo).
Axes of the slice: x: 4, y: 4, z: 4 (z_hi: 2, z_lo: 2; z = z_hi * 2 + z_lo), core: 2. Of those that a mesh axis runs over, the one named last changes fastest.
Arguments:
- first_features: bfloat16 [256, 128, 128], P(('pair', 'row'), 'col'), parts along dimension 0, may hold values from -20 to 20
- second_features: bfloat16 [256, 128, 128], P(('pair', 'row'), 'col'), parts along dimension 0, may hold values from -20 to 20
- attend_weight: bfloat16 [128, 384], replicated, may hold values from -0.5 to 0.5
- merge_weight: bfloat16 [128, 128], replicated, may hold values from -0.5 to 0.5
- message_gain: float32 [128], replicated, may hold values from 0.3 to 1.7
- message_bias: float32 [128], replicated, may hold values from -3 to 3
- expand_weight: bfloat16 [256, 1024], replicated, may hold values from -0.375 to 0.375
- reduce_weight: bfloat16 [1024, 128], replicated, may hold values from -0.1875 to 0.1875
- update_gain: float32 [128], replicated, may hold values from 0.5 to 1.5
- update_bias: float32 [128], replicated, may hold values from -3 to 3
Outputs:
- flow_field: float32 [2, 256, 128], P(None, ('pair', 'row'), 'col'), parts along dimension 1
There are 2 independent parts, one for each index of `pair`. A program takes and returns all parts, laid end to end along the dimension named above; an argument that names none is the same for every part. Nothing has to cross between parts.
All inputs are finite; a program needn't handle non-finite values.
Results may differ from a plain program's by a relative error of at most 0.019.
Values may be sent and summed in bfloat16 or wider, within the bound.
A program may use at most 64 MiB of HBM per device.

v0:
```python
import math

import jax
import jax.numpy as jnp
from jax import lax
from jax.sharding import PartitionSpec as P

HEADS = 8
SPLITS = 2
HEAD_DIM = 16


NORM_EPSILON = 1e-05
MASKED = -1e30


def passed_along(x, axis, by):
    length = lax.axis_size(axis)
    pairs = [(i, i + by) for i in range(length) if 0 <= i + by < length]
    return lax.ppermute(x, axis, pairs)


def layer_norm(values, scale_by, shift_by):
    centre = values - jnp.mean(values, axis=-1, keepdims=True)
    spread = jnp.mean(centre * centre, axis=-1, keepdims=True)
    return centre * lax.rsqrt(spread + NORM_EPSILON) * scale_by + shift_by


def make_window_fold(
    queries,
    query_row_label,
    query_column_label,
    cell_count,
    band_rows,
    strip_width,
    row_count,
    window_rows,
    window_columns,
):
    head_scale = 1.0 / math.sqrt(HEAD_DIM)

    def accumulate(state, piece, source_band):
        piece_cells = piece.shape[1]
        cell_index = jnp.arange(piece_cells, dtype=jnp.int32)
        strip_at = cell_index // cell_count
        within = cell_index % cell_count
        key_row = band_rows * source_band + within // strip_width
        key_column = strip_width * strip_at + within % strip_width
        key_row_label = (key_row + window_rows // 2) // window_rows
        key_column_label = (key_column + window_columns // 2) // window_columns
        present = (source_band >= 0) & (source_band < row_count)
        allowed = (
            (query_row_label[:, None] == key_row_label[None, :])
            & (query_column_label[:, None] == key_column_label[None, :])
            & present
        )

        def update(state_in):
            run_max, run_sum, run_acc = state_in
            half = piece.shape[2] // 2
            key_part = piece[:, :, :half].reshape(2, piece_cells, HEADS, HEAD_DIM)
            value_part = piece[:, :, half:].reshape(2, piece_cells, HEADS, HEAD_DIM)
            scores = (
                jnp.einsum("fqhd,fkhd->fhqk", queries, key_part, preferred_element_type=jnp.float32)
                * head_scale
            )
            scores = jnp.where(allowed[None, None], scores, MASKED)
            new_max = jnp.maximum(run_max, jnp.max(scores, axis=-1))
            lifted = jnp.where(allowed[None, None], jnp.exp(scores - new_max[..., None]), 0.0)
            rescale = jnp.exp(run_max - new_max)
            new_sum = run_sum * rescale + jnp.sum(lifted, axis=-1)
            product = jnp.einsum(
                "fhqk,fkhd->fhqd",
                lifted.astype(jnp.bfloat16),
                value_part,
                preferred_element_type=jnp.float32,
            )
            new_acc = run_acc * rescale[..., None] + product
            return (new_max, new_sum, new_acc)

        return lax.cond(jnp.any(allowed), update, lambda state_in: state_in, state)

    return accumulate


def make_fold(queries, band_rows, strip_width, column_count):
    score_scale = 1.0 / math.sqrt(queries.shape[1])
    cell_count = band_rows * strip_width

    def accumulate(running, incoming, first_row):
        run_max, run_sum, sum_column, sum_row = running
        piece_rows = incoming.shape[0]
        cell_index = jnp.arange(piece_rows, dtype=jnp.int32)
        device = cell_index // cell_count
        within = cell_index % cell_count
        source_row = band_rows * (device // column_count) + within // strip_width
        source_column = strip_width * (device % column_count) + within % strip_width
        scores = (
            lax.dot_general(
                queries, incoming, (((1,), (1,)), ((), ())), preferred_element_type=jnp.float32
            )
            * score_scale
        )
        new_max = jnp.maximum(run_max, jnp.max(scores, axis=1))
        lifted = jnp.exp(scores - new_max[:, None])
        run_sum = jnp.sum(lifted, axis=1)
        sum_column = jnp.sum(lifted * source_column.astype(jnp.float32)[None, :], axis=1)
        sum_row = jnp.sum(lifted * source_row.astype(jnp.float32)[None, :], axis=1)
        return (new_max, run_sum, sum_column, sum_row)

    return accumulate


def shards(
    first_features,
    second_features,
    attend_weight,
    merge_weight,
    message_gain,
    message_bias,
    expand_weight,
    reduce_weight,
    update_gain,
    update_bias,
):
    band_rows, strip_width, channels = first_features.shape
    row_count = lax.axis_size("row")
    column_count = lax.axis_size("col")
    rows_total = band_rows * row_count
    columns_total = strip_width * column_count
    window_rows = rows_total // SPLITS
    window_columns = columns_total // SPLITS
    row_at = lax.axis_index("row")
    column_at = lax.axis_index("col")
    cell_count = band_rows * strip_width
    frames = jnp.stack([first_features, second_features]).reshape(2, cell_count, channels)
    flat_frames = frames.reshape(-1, channels)
    queries = jnp.dot(flat_frames, attend_weight[:, :channels], preferred_element_type=jnp.float32)
    queries = queries.astype(jnp.bfloat16).reshape(2, cell_count, HEADS, HEAD_DIM)
    own_rows = row_at * band_rows + jnp.arange(band_rows, dtype=jnp.int32)
    own_columns = column_at * strip_width + jnp.arange(strip_width, dtype=jnp.int32)
    row_flat = jnp.broadcast_to(own_rows[:, None], (band_rows, strip_width)).reshape(-1)
    column_flat = jnp.broadcast_to(own_columns[None, :], (band_rows, strip_width)).reshape(-1)
    query_row_label = (row_flat + window_rows // 2) // window_rows
    query_column_label = (column_flat + window_columns // 2) // window_columns
    window_fold = make_window_fold(
        queries,
        query_row_label,
        query_column_label,
        cell_count,
        band_rows,
        strip_width,
        row_count,
        window_rows,
        window_columns,
    )
    start_state = (
        jnp.full((2, HEADS, cell_count), MASKED, jnp.float32),
        jnp.zeros((2, HEADS, cell_count), jnp.float32),
        jnp.zeros((2, HEADS, cell_count, HEAD_DIM), jnp.float32),
    )
    keyval = jnp.dot(flat_frames, attend_weight[:, channels:], preferred_element_type=jnp.float32)
    keyval = keyval.astype(jnp.bfloat16).reshape(2, cell_count, 2 * channels)
    widened = lax.all_gather(keyval, "col", axis=1, tiled=True)
    state = window_fold(start_state, widened, row_at)
    reach = min(row_count - 1, (window_rows + band_rows - 2) // band_rows)

    def turn(step, carry):
        state_in, below, above = carry
        below = passed_along(below, "row", 1)
        above = passed_along(above, "row", -1)
        state_in = window_fold(state_in, below, row_at - step - 1)
        state_in = window_fold(state_in, above, row_at + step + 1)
        return (state_in, below, above)

    state, below_last, above_last = lax.fori_loop(0, reach, turn, (state, widened, widened))
    run_max, run_total, run_acc = state
    attended = (run_acc / run_total[..., None]).astype(jnp.bfloat16)
    attended = attended.transpose(0, 2, 1, 3).reshape(-1, channels)
    message = layer_norm(
        jnp.dot(attended, merge_weight, preferred_element_type=jnp.float32),
        message_gain,
        message_bias,
    ).astype(jnp.bfloat16)
    expanded = jnp.dot(flat_frames, expand_weight[:channels], preferred_element_type=jnp.float32)
    expanded = expanded + jnp.dot(
        message, expand_weight[channels:], preferred_element_type=jnp.float32
    )
    hidden = jax.nn.gelu(expanded, approximate=False).astype(jnp.bfloat16)
    update = layer_norm(
        jnp.dot(hidden, reduce_weight, preferred_element_type=jnp.float32), update_gain, update_bias
    )
    refined = (
        (flat_frames.astype(jnp.float32) + update)
        .astype(jnp.bfloat16)
        .reshape(2, cell_count, channels)
    )
    first_refined = refined[0]
    second_cells = refined[1]
    accumulate = make_fold(first_refined, band_rows, strip_width, column_count)
    initial = (
        jnp.full((cell_count,), MASKED, jnp.float32),
        jnp.zeros((cell_count,), jnp.float32),
        jnp.zeros((cell_count,), jnp.float32),
        jnp.zeros((cell_count,), jnp.float32),
    )
    gathered = accumulate(
        initial, lax.all_gather(second_cells, ("row", "col"), axis=0, tiled=True), jnp.int32(0)
    )
    corr_max, corr_sum, sum_column, sum_row = gathered
    flow_column = (sum_column / corr_sum - column_flat.astype(jnp.float32)) * (2.0 / columns_total)
    flow_row = (sum_row / corr_sum - row_flat.astype(jnp.float32)) * (2.0 / rows_total)
    return jnp.stack([flow_column, flow_row]).reshape(2, band_rows, strip_width)


def solution(mesh):
    return jax.shard_map(
        shards,
        mesh=mesh,
        in_specs=(
            P(("pair", "row"), "col", None),
            P(("pair", "row"), "col", None),
            P(),
            P(),
            P(),
            P(),
            P(),
            P(),
            P(),
            P(),
        ),
        out_specs=P(None, ("pair", "row"), "col"),
        check_vma=False,
    )
```

profile of v0, /device:TPU:1, one launch (start us, length us, event | category | flops | bytes accessed | tf_op | source)
XLA Modules:
  0.0 593.9 jit_solution(5556660964663800358)
XLA Ops:
  10.0 9.1 %all_gather.6 = bf16[2,512,256]{1,2,0:T(8,128)(2,1)S(1)} all-gather(bf16[2,256,256]{1,2,0:T(8,128)(2,1)S(1)} %copy.16), channel_id=1, replica_groups=mesh['pair'=2,'row'=32,'col'=2] {'col'}, dimensions={1}, use_global_device_ids=true | all-gather | bytes 786432 | tf_op jit(solution)/shard_map/all_gather | solution.py:164
  21.0 9.1 %conditional.3 = (f32[2,8,256]{2,1,0:T(8,128)}, f32[2,8,256]{2,1,0:T(8,128)S(1)}, f32[2,8,256,16]{2,3,1,0:T(8,128)S(1)}) conditional(s32[]{:T(128)} %convert_element_type.82, () %tuple.51, (pred[256,512]{1,0:T(8,128)(4,1)S(1)}, bf16[2,512,256]{1,2,0:T(8,128)(2,1)S(1)}, bf16[2,256,8,16]{1,0,3,2:T(2,128)(2,1)S(1)}) %tuple.52), branch_computations={%region_1.2_spmd, %region_2.5_spmd} | conditional | flops 161562624 | bytes 27705368 | solution.py:81
  30.1 361.8 %while.25 = (s32[]{:T(128)}, f32[2,8,256]{2,1,0:T(8,128)}, f32[2,8,256]{2,1,0:T(8,128)S(1)}, f32[2,8,256,16]{2,3,1,0:T(8,128)S(1)}, bf16[2,512,256]{1,2,0:T(8,12...) while((s32[]{:T(128)}, f32[2,8,256]{2,1,0:T(8,128)}, ...), condition=%wide.region_16.17_spmd.clone, body=%wide.region_5.16_spmd.clone.sunk | while | flops 324480512 | bytes 62677804 | solution.py:176
  30.1 4.4 collective-permute-start
  40.5 8.2 %conditional.8 = ((f32[2,8,256]{2,1,0:T(8,128)}, f32[2,8,256]{2,1,0:T(8,128)S(1)}, f32[2,8,256,16]{2,3,1,0:T(8,128)S(1)})) conditional(s32[]{:T(128)} %convert_element_type.131, (f32[2,8,256]{2,1,0:T(8,128)}, f32[2,8,256]{2,1,0:T(8,128)S(1)}, f32[2,8,256,16]{2,3,1,0:T(8,128)S(1)}) %tuple.106, (pred[256,512]{1,0:T(8,128)(4,1)S(1)}, ...), branch_computations={%region_8.8_spmd, %region_9.11_spmd} | conditional | flops 161619968 | bytes 28049440 | solution.py:81
  48.7 8.2 %conditional.9 = ((f32[2,8,256]{2,1,0:T(8,128)}, f32[2,8,256]{2,1,0:T(8,128)S(1)}, f32[2,8,256,16]{2,3,1,0:T(8,128)S(1)})) conditional(s32[]{:T(128)} %convert_element_type.130, (f32[2,8,256]{2,1,0:T(8,128)}, f32[2,8,256]{2,1,0:T(8,128)S(1)}, f32[2,8,256,16]{2,3,1,0:T(8,128)S(1)}) %get-tuple-element.661, (pred[256,512]{1,0:T(8,128)(4,1)S(1)}, ...), branch_computations={%region_12.12_spmd, %region_13.15_spmd} | conditional | flops 161619968 | bytes 28049440 | solution.py:81
  57.0 4.4 collective-permute-start
  67.5 4.4 collective-permute-done.1
  71.9 8.2 %conditional.9 = ((f32[2,8,256]{2,1,0:T(8,128)}, f32[2,8,256]{2,1,0:T(8,128)S(1)}, f32[2,8,256,16]{2,3,1,0:T(8,128)S(1)})) conditional(s32[]{:T(128)} %convert_element_type.130, (f32[2,8,256]{2,1,0:T(8,128)}, f32[2,8,256]{2,1,0:T(8,128)S(1)}, f32[2,8,256,16]{2,3,1,0:T(8,128)S(1)}) %get-tuple-element.661, (pred[256,512]{1,0:T(8,128)(4,1)S(1)}, ...), branch_computations={%region_12.12_spmd, %region_13.15_spmd} | conditional | flops 161619968 | bytes 28049440 | solution.py:81
  80.1 8.2 %collective-permute-start = (bf16[2,512,256]{1,2,0:T(8,128)(2,1)S(1)}, bf16[2,512,256]{1,2,0:T(8,128)(2,1)S(1)}, u32[]{:S(2)}, u32[]{:S(2)}) collective-permute-start(bf16[2,512,256]{1,2,0:T(8,128)(2,1)S(1)} %get-tuple-element.635), channel_id=1, source_target_pairs={{0,2},{2,4},{4,6},{6,8},{8,10},{10,12},{12,14},{14,16},{16,18},{18... | collective-permute-start | bytes 1572872 | tf_op jit(solution)/shard_map/while/body/eval_jaxpr/ppermute | solution.py:20
  94.4 4.4 collective-permute-done.1
  98.8 8.2 %conditional.9 = ((f32[2,8,256]{2,1,0:T(8,128)}, f32[2,8,256]{2,1,0:T(8,128)S(1)}, f32[2,8,256,16]{2,3,1,0:T(8,128)S(1)})) conditional(s32[]{:T(128)} %convert_element_type.130, (f32[2,8,256]{2,1,0:T(8,128)}, f32[2,8,256]{2,1,0:T(8,128)S(1)}, f32[2,8,256,16]{2,3,1,0:T(8,128)S(1)}) %get-tuple-element.661, (pred[256,512]{1,0:T(8,128)(4,1)S(1)}, ...), branch_computations={%region_12.12_spmd, %region_13.15_spmd} | conditional | flops 161619968 | bytes 28049440 | solution.py:81
  115.1 8.1 %collective-permute-done.1 = bf16[2,512,256]{1,2,0:T(8,128)(2,1)S(1)} collective-permute-done((bf16[2,512,256]{1,2,0:T(8,128)(2,1)S(1)}, bf16[2,512,256]{1,2,0:T(8,128)(2,1)S(1)}, u32[]{:S(2)}, u32[]{:S(2)}) %collective-permute-start.1) | collective-permute-done | bytes 524320 | tf_op jit(solution)/shard_map/while/body/eval_jaxpr/ppermute | solution.py:20
  123.2 8.2 %conditional.9 = ((f32[2,8,256]{2,1,0:T(8,128)}, f32[2,8,256]{2,1,0:T(8,128)S(1)}, f32[2,8,256,16]{2,3,1,0:T(8,128)S(1)})) conditional(s32[]{:T(128)} %convert_element_type.130, (f32[2,8,256]{2,1,0:T(8,128)}, f32[2,8,256]{2,1,0:T(8,128)S(1)}, f32[2,8,256,16]{2,3,1,0:T(8,128)S(1)}) %get-tuple-element.661, (pred[256,512]{1,0:T(8,128)(4,1)S(1)}, ...), branch_computations={%region_12.12_spmd, %region_13.15_spmd} | conditional | flops 161619968 | bytes 28049440 | solution.py:81
  139.5 6.9 %collective-permute-done.1 = bf16[2,512,256]{1,2,0:T(8,128)(2,1)S(1)} collective-permute-done((bf16[2,512,256]{1,2,0:T(8,128)(2,1)S(1)}, bf16[2,512,256]{1,2,0:T(8,128)(2,1)S(1)}, u32[]{:S(2)}, u32[]{:S(2)}) %collective-permute-start.1) | collective-permute-done | bytes 524320 | tf_op jit(solution)/shard_map/while/body/eval_jaxpr/ppermute | solution.py:20
  146.4 8.2 %conditional.9 = ((f32[2,8,256]{2,1,0:T(8,128)}, f32[2,8,256]{2,1,0:T(8,128)S(1)}, f32[2,8,256,16]{2,3,1,0:T(8,128)S(1)})) conditional(s32[]{:T(128)} %convert_element_type.130, (f32[2,8,256]{2,1,0:T(8,128)}, f32[2,8,256]{2,1,0:T(8,128)S(1)}, f32[2,8,256,16]{2,3,1,0:T(8,128)S(1)}) %get-tuple-element.661, (pred[256,512]{1,0:T(8,128)(4,1)S(1)}, ...), branch_computations={%region_12.12_spmd, %region_13.15_spmd} | conditional | flops 161619968 | bytes 28049440 | solution.py:81
  162.7 4.4 collective-permute-done.1
  167.1 8.2 %conditional.9 = ((f32[2,8,256]{2,1,0:T(8,128)}, f32[2,8,256]{2,1,0:T(8,128)S(1)}, f32[2,8,256,16]{2,3,1,0:T(8,128)S(1)})) conditional(s32[]{:T(128)} %convert_element_type.130, (f32[2,8,256]{2,1,0:T(8,128)}, f32[2,8,256]{2,1,0:T(8,128)S(1)}, f32[2,8,256,16]{2,3,1,0:T(8,128)S(1)}) %get-tuple-element.661, (pred[256,512]{1,0:T(8,128)(4,1)S(1)}, ...), branch_computations={%region_12.12_spmd, %region_13.15_spmd} | conditional | flops 161619968 | bytes 28049440 | solution.py:81
  183.4 4.4 collective-permute-done.1
  195.9 4.4 collective-permute-done.1
  208.4 4.4 collective-permute-done.1
  220.9 10.0 %collective-permute-done.1 = bf16[2,512,256]{1,2,0:T(8,128)(2,1)S(1)} collective-permute-done((bf16[2,512,256]{1,2,0:T(8,128)(2,1)S(1)}, bf16[2,512,256]{1,2,0:T(8,128)(2,1)S(1)}, u32[]{:S(2)}, u32[]{:S(2)}) %collective-permute-start.1) | collective-permute-done | bytes 524320 | tf_op jit(solution)/shard_map/while/body/eval_jaxpr/ppermute | solution.py:20
  239.1 15.7 %collective-permute-done.1 = bf16[2,512,256]{1,2,0:T(8,128)(2,1)S(1)} collective-permute-done((bf16[2,512,256]{1,2,0:T(8,128)(2,1)S(1)}, bf16[2,512,256]{1,2,0:T(8,128)(2,1)S(1)}, u32[]{:S(2)}, u32[]{:S(2)}) %collective-permute-start.1) | collective-permute-done | bytes 524320 | tf_op jit(solution)/shard_map/while/body/eval_jaxpr/ppermute | solution.py:20
  262.9 20.5 %collective-permute-done.1 = bf16[2,512,256]{1,2,0:T(8,128)(2,1)S(1)} collective-permute-done((bf16[2,512,256]{1,2,0:T(8,128)(2,1)S(1)}, bf16[2,512,256]{1,2,0:T(8,128)(2,1)S(1)}, u32[]{:S(2)}, u32[]{:S(2)}) %collective-permute-start.1) | collective-permute-done | bytes 524320 | tf_op jit(solution)/shard_map/while/body/eval_jaxpr/ppermute | solution.py:20
  291.5 20.9 %collective-permute-done.1 = bf16[2,512,256]{1,2,0:T(8,128)(2,1)S(1)} collective-permute-done((bf16[2,512,256]{1,2,0:T(8,128)(2,1)S(1)}, bf16[2,512,256]{1,2,0:T(8,128)(2,1)S(1)}, u32[]{:S(2)}, u32[]{:S(2)}) %collective-permute-start.1) | collective-permute-done | bytes 524320 | tf_op jit(solution)/shard_map/while/body/eval_jaxpr/ppermute | solution.py:20
  320.6 20.9 %collective-permute-done.1 = bf16[2,512,256]{1,2,0:T(8,128)(2,1)S(1)} collective-permute-done((bf16[2,512,256]{1,2,0:T(8,128)(2,1)S(1)}, bf16[2,512,256]{1,2,0:T(8,128)(2,1)S(1)}, u32[]{:S(2)}, u32[]{:S(2)}) %collective-permute-start.1) | collective-permute-done | bytes 524320 | tf_op jit(solution)/shard_map/while/body/eval_jaxpr/ppermute | solution.py:20
  349.6 19.2 %collective-permute-done.1 = bf16[2,512,256]{1,2,0:T(8,128)(2,1)S(1)} collective-permute-done((bf16[2,512,256]{1,2,0:T(8,128)(2,1)S(1)}, bf16[2,512,256]{1,2,0:T(8,128)(2,1)S(1)}, u32[]{:S(2)}, u32[]{:S(2)}) %collective-permute-start.1) | collective-permute-done | bytes 524320 | tf_op jit(solution)/shard_map/while/body/eval_jaxpr/ppermute | solution.py:20
  377.0 14.5 %collective-permute-done.1 = bf16[2,512,256]{1,2,0:T(8,128)(2,1)S(1)} collective-permute-done((bf16[2,512,256]{1,2,0:T(8,128)(2,1)S(1)}, bf16[2,512,256]{1,2,0:T(8,128)(2,1)S(1)}, u32[]{:S(2)}, u32[]{:S(2)}) %collective-permute-start.1) | collective-permute-done | bytes 524320 | tf_op jit(solution)/shard_map/while/body/eval_jaxpr/ppermute | solution.py:20
  393.8 6.3 %fusion.202 = (f32[512]{0:T(512)S(1)}, f32[512,128]{0,1:T(8,128)S(1)}) fusion(bf16[1024,128]{1,0:T(8,128)(2,1)S(1)} %copy-done, f32[512,1024]{1,0:T(8,128)S(1)} %fusion.105, bf16[256,1024]{1,0:T(8,128)(2,1)} %param.24, f32[512,128]{0,1:T(8,128)S(1)} %get-tuple-element.498, f32[128]{0:T(128)S(1)} %copy-done.4, f32[128]{0:T(128)S(1)} %copy-done.5, ...), kind=kOutput, calls=%fused_computation.311 | convolution fusion | flops 303431168 | bytes 3152896 | tf_op jit(solution)/shard_map/dot_general | solution.py:191
  401.1 174.6 %all-gather.2.cloned.1.call-done = bf16[16384,128]{0,1:T(8,128)(2,1)} async-done(((bf16[256,128]{0,1:T(8,128)(2,1)}), bf16[16384,128]{0,1:T(8,128)(2,1)}) %all-gather.2.cloned.1.call-update) | async-done | bytes 4194320 | tf_op jit(solution)/shard_map/all_gather | solution.py:208
  575.7 4.7 fusion.205
  580.4 5.8 multiply_reduce_fusion.1
  (341 shorter events, 177.1 us)
Async XLA Ops:
  6.5 569.2 %all-gather.2.cloned.1.call-start = ((), (), s32[]{:S(2)}) async-start(), calls=%async_computation | async-start | bytes 4259840 | tf_op jit(solution)/shard_map/all_gather | solution.py:208
  30.1 10.5 %collective-permute-start = (bf16[2,512,256]{1,2,0:T(8,128)(2,1)S(1)}, bf16[2,512,256]{1,2,0:T(8,128)(2,1)S(1)}, u32[]{:S(2)}, u32[]{:S(2)}) collective-permute-start(bf16[2,512,256]{1,2,0:T(8,128)(2,1)S(1)} %get-tuple-element.635), channel_id=1, source_target_pairs={{0,2},{2,4},{4,6},{6,8},{8,10},{10,12},{12,14},{14,16},{16,18},{18... | collective-permute-start | bytes 1572872 | tf_op jit(solution)/shard_map/while/body/eval_jaxpr/ppermute | solution.py:20
  34.4 14.3 %collective-permute-start.1 = (bf16[2,512,256]{1,2,0:T(8,128)(2,1)S(1)}, bf16[2,512,256]{1,2,0:T(8,128)(2,1)S(1)}, u32[]{:S(2)}, u32[]{:S(2)}) collective-permute-start(bf16[2,512,256]{1,2,0:T(8,128)(2,1)S(1)} %get-tuple-element.636), channel_id=1, source_target_pairs={{2,0},{4,2},{6,4},{8,6},{10,8},{12,10},{14,12},{16,14},{18,16},{20... | collective-permute-start | bytes 1572872 | tf_op jit(solution)/shard_map/while/body/eval_jaxpr/ppermute | solution.py:20
  57.0 10.5 %collective-permute-start = (bf16[2,512,256]{1,2,0:T(8,128)(2,1)S(1)}, bf16[2,512,256]{1,2,0:T(8,128)(2,1)S(1)}, u32[]{:S(2)}, u32[]{:S(2)}) collective-permute-start(bf16[2,512,256]{1,2,0:T(8,128)(2,1)S(1)} %get-tuple-element.635), channel_id=1, source_target_pairs={{0,2},{2,4},{4,6},{6,8},{8,10},{10,12},{12,14},{14,16},{16,18},{18... | collective-permute-start | bytes 1572872 | tf_op jit(solution)/shard_map/while/body/eval_jaxpr/ppermute | solution.py:20
  61.4 10.5 %collective-permute-start.1 = (bf16[2,512,256]{1,2,0:T(8,128)(2,1)S(1)}, bf16[2,512,256]{1,2,0:T(8,128)(2,1)S(1)}, u32[]{:S(2)}, u32[]{:S(2)}) collective-permute-start(bf16[2,512,256]{1,2,0:T(8,128)(2,1)S(1)} %get-tuple-element.636), channel_id=1, source_target_pairs={{2,0},{4,2},{6,4},{8,6},{10,8},{12,10},{14,12},{16,14},{18,16},{20... | collective-permute-start | bytes 1572872 | tf_op jit(solution)/shard_map/while/body/eval_jaxpr/ppermute | solution.py:20
  80.1 14.3 %collective-permute-start = (bf16[2,512,256]{1,2,0:T(8,128)(2,1)S(1)}, bf16[2,512,256]{1,2,0:T(8,128)(2,1)S(1)}, u32[]{:S(2)}, u32[]{:S(2)}) collective-permute-start(bf16[2,512,256]{1,2,0:T(8,128)(2,1)S(1)} %get-tuple-element.635), channel_id=1, source_target_pairs={{0,2},{2,4},{4,6},{6,8},{8,10},{10,12},{12,14},{14,16},{16,18},{18... | collective-permute-start | bytes 1572872 | tf_op jit(solution)/shard_map/while/body/eval_jaxpr/ppermute | solution.py:20
  88.3 10.5 %collective-permute-start.1 = (bf16[2,512,256]{1,2,0:T(8,128)(2,1)S(1)}, bf16[2,512,256]{1,2,0:T(8,128)(2,1)S(1)}, u32[]{:S(2)}, u32[]{:S(2)}) collective-permute-start(bf16[2,512,256]{1,2,0:T(8,128)(2,1)S(1)} %get-tuple-element.636), channel_id=1, source_target_pairs={{2,0},{4,2},{6,4},{8,6},{10,8},{12,10},{14,12},{16,14},{18,16},{20... | collective-permute-start | bytes 1572872 | tf_op jit(solution)/shard_map/while/body/eval_jaxpr/ppermute | solution.py:20
  107.1 8.0 %collective-permute-start = (bf16[2,512,256]{1,2,0:T(8,128)(2,1)S(1)}, bf16[2,512,256]{1,2,0:T(8,128)(2,1)S(1)}, u32[]{:S(2)}, u32[]{:S(2)}) collective-permute-start(bf16[2,512,256]{1,2,0:T(8,128)(2,1)S(1)} %get-tuple-element.635), channel_id=1, source_target_pairs={{0,2},{2,4},{4,6},{6,8},{8,10},{10,12},{12,14},{14,16},{16,18},{18... | collective-permute-start | bytes 1572872 | tf_op jit(solution)/shard_map/while/body/eval_jaxpr/ppermute | solution.py:20
  109.0 14.2 %collective-permute-start.1 = (bf16[2,512,256]{1,2,0:T(8,128)(2,1)S(1)}, bf16[2,512,256]{1,2,0:T(8,128)(2,1)S(1)}, u32[]{:S(2)}, u32[]{:S(2)}) collective-permute-start(bf16[2,512,256]{1,2,0:T(8,128)(2,1)S(1)} %get-tuple-element.636), channel_id=1, source_target_pairs={{2,0},{4,2},{6,4},{8,6},{10,8},{12,10},{14,12},{16,14},{18,16},{20... | collective-permute-start | bytes 1572872 | tf_op jit(solution)/shard_map/while/body/eval_jaxpr/ppermute | solution.py:20
  131.5 8.0 %collective-permute-start = (bf16[2,512,256]{1,2,0:T(8,128)(2,1)S(1)}, bf16[2,512,256]{1,2,0:T(8,128)(2,1)S(1)}, u32[]{:S(2)}, u32[]{:S(2)}) collective-permute-start(bf16[2,512,256]{1,2,0:T(8,128)(2,1)S(1)} %get-tuple-element.635), channel_id=1, source_target_pairs={{0,2},{2,4},{4,6},{6,8},{8,10},{10,12},{12,14},{14,16},{16,18},{18... | collective-permute-start | bytes 1572872 | tf_op jit(solution)/shard_map/while/body/eval_jaxpr/ppermute | solution.py:20
  133.4 13.0 %collective-permute-start.1 = (bf16[2,512,256]{1,2,0:T(8,128)(2,1)S(1)}, bf16[2,512,256]{1,2,0:T(8,128)(2,1)S(1)}, u32[]{:S(2)}, u32[]{:S(2)}) collective-permute-start(bf16[2,512,256]{1,2,0:T(8,128)(2,1)S(1)} %get-tuple-element.636), channel_id=1, source_target_pairs={{2,0},{4,2},{6,4},{8,6},{10,8},{12,10},{14,12},{16,14},{18,16},{20... | collective-permute-start | bytes 1572872 | tf_op jit(solution)/shard_map/while/body/eval_jaxpr/ppermute | solution.py:20
  154.6 8.0 %collective-permute-start = (bf16[2,512,256]{1,2,0:T(8,128)(2,1)S(1)}, bf16[2,512,256]{1,2,0:T(8,128)(2,1)S(1)}, u32[]{:S(2)}, u32[]{:S(2)}) collective-permute-start(bf16[2,512,256]{1,2,0:T(8,128)(2,1)S(1)} %get-tuple-element.635), channel_id=1, source_target_pairs={{0,2},{2,4},{4,6},{6,8},{8,10},{10,12},{12,14},{14,16},{16,18},{18... | collective-permute-start | bytes 1572872 | tf_op jit(solution)/shard_map/while/body/eval_jaxpr/ppermute | solution.py:20
  156.6 10.5 %collective-permute-start.1 = (bf16[2,512,256]{1,2,0:T(8,128)(2,1)S(1)}, bf16[2,512,256]{1,2,0:T(8,128)(2,1)S(1)}, u32[]{:S(2)}, u32[]{:S(2)}) collective-permute-start(bf16[2,512,256]{1,2,0:T(8,128)(2,1)S(1)} %get-tuple-element.636), channel_id=1, source_target_pairs={{2,0},{4,2},{6,4},{8,6},{10,8},{12,10},{14,12},{16,14},{18,16},{20... | collective-permute-start | bytes 1572872 | tf_op jit(solution)/shard_map/while/body/eval_jaxpr/ppermute | solution.py:20
  175.3 8.0 %collective-permute-start = (bf16[2,512,256]{1,2,0:T(8,128)(2,1)S(1)}, bf16[2,512,256]{1,2,0:T(8,128)(2,1)S(1)}, u32[]{:S(2)}, u32[]{:S(2)}) collective-permute-start(bf16[2,512,256]{1,2,0:T(8,128)(2,1)S(1)} %get-tuple-element.635), channel_id=1, source_target_pairs={{0,2},{2,4},{4,6},{6,8},{8,10},{10,12},{12,14},{14,16},{16,18},{18... | collective-permute-start | bytes 1572872 | tf_op jit(solution)/shard_map/while/body/eval_jaxpr/ppermute | solution.py:20
  177.3 10.5 %collective-permute-start.1 = (bf16[2,512,256]{1,2,0:T(8,128)(2,1)S(1)}, bf16[2,512,256]{1,2,0:T(8,128)(2,1)S(1)}, u32[]{:S(2)}, u32[]{:S(2)}) collective-permute-start(bf16[2,512,256]{1,2,0:T(8,128)(2,1)S(1)} %get-tuple-element.636), channel_id=1, source_target_pairs={{2,0},{4,2},{6,4},{8,6},{10,8},{12,10},{14,12},{16,14},{18,16},{20... | collective-permute-start | bytes 1572872 | tf_op jit(solution)/shard_map/while/body/eval_jaxpr/ppermute | solution.py:20
  187.9 8.0 %collective-permute-start = (bf16[2,512,256]{1,2,0:T(8,128)(2,1)S(1)}, bf16[2,512,256]{1,2,0:T(8,128)(2,1)S(1)}, u32[]{:S(2)}, u32[]{:S(2)}) collective-permute-start(bf16[2,512,256]{1,2,0:T(8,128)(2,1)S(1)} %get-tuple-element.635), channel_id=1, source_target_pairs={{0,2},{2,4},{4,6},{6,8},{8,10},{10,12},{12,14},{14,16},{16,18},{18... | collective-permute-start | bytes 1572872 | tf_op jit(solution)/shard_map/while/body/eval_jaxpr/ppermute | solution.py:20
  189.8 10.5 %collective-permute-start.1 = (bf16[2,512,256]{1,2,0:T(8,128)(2,1)S(1)}, bf16[2,512,256]{1,2,0:T(8,128)(2,1)S(1)}, u32[]{:S(2)}, u32[]{:S(2)}) collective-permute-start(bf16[2,512,256]{1,2,0:T(8,128)(2,1)S(1)} %get-tuple-element.636), channel_id=1, source_target_pairs={{2,0},{4,2},{6,4},{8,6},{10,8},{12,10},{14,12},{16,14},{18,16},{20... | collective-permute-start | bytes 1572872 | tf_op jit(solution)/shard_map/while/body/eval_jaxpr/ppermute | solution.py:20
  200.4 8.0 %collective-permute-start = (bf16[2,512,256]{1,2,0:T(8,128)(2,1)S(1)}, bf16[2,512,256]{1,2,0:T(8,128)(2,1)S(1)}, u32[]{:S(2)}, u32[]{:S(2)}) collective-permute-start(bf16[2,512,256]{1,2,0:T(8,128)(2,1)S(1)} %get-tuple-element.635), channel_id=1, source_target_pairs={{0,2},{2,4},{4,6},{6,8},{8,10},{10,12},{12,14},{14,16},{16,18},{18... | collective-permute-start | bytes 1572872 | tf_op jit(solution)/shard_map/while/body/eval_jaxpr/ppermute | solution.py:20
  202.3 10.5 %collective-permute-start.1 = (bf16[2,512,256]{1,2,0:T(8,128)(2,1)S(1)}, bf16[2,512,256]{1,2,0:T(8,128)(2,1)S(1)}, u32[]{:S(2)}, u32[]{:S(2)}) collective-permute-start(bf16[2,512,256]{1,2,0:T(8,128)(2,1)S(1)} %get-tuple-element.636), channel_id=1, source_target_pairs={{2,0},{4,2},{6,4},{8,6},{10,8},{12,10},{14,12},{16,14},{18,16},{20... | collective-permute-start | bytes 1572872 | tf_op jit(solution)/shard_map/while/body/eval_jaxpr/ppermute | solution.py:20
  212.9 8.0 %collective-permute-start = (bf16[2,512,256]{1,2,0:T(8,128)(2,1)S(1)}, bf16[2,512,256]{1,2,0:T(8,128)(2,1)S(1)}, u32[]{:S(2)}, u32[]{:S(2)}) collective-permute-start(bf16[2,512,256]{1,2,0:T(8,128)(2,1)S(1)} %get-tuple-element.635), channel_id=1, source_target_pairs={{0,2},{2,4},{4,6},{6,8},{8,10},{10,12},{12,14},{14,16},{16,18},{18... | collective-permute-start | bytes 1572872 | tf_op jit(solution)/shard_map/while/body/eval_jaxpr/ppermute | solution.py:20
  214.8 16.1 %collective-permute-start.1 = (bf16[2,512,256]{1,2,0:T(8,128)(2,1)S(1)}, bf16[2,512,256]{1,2,0:T(8,128)(2,1)S(1)}, u32[]{:S(2)}, u32[]{:S(2)}) collective-permute-start(bf16[2,512,256]{1,2,0:T(8,128)(2,1)S(1)} %get-tuple-element.636), channel_id=1, source_target_pairs={{2,0},{4,2},{6,4},{8,6},{10,8},{12,10},{14,12},{16,14},{18,16},{20... | collective-permute-start | bytes 1572872 | tf_op jit(solution)/shard_map/while/body/eval_jaxpr/ppermute | solution.py:20
  231.0 8.0 %collective-permute-start = (bf16[2,512,256]{1,2,0:T(8,128)(2,1)S(1)}, bf16[2,512,256]{1,2,0:T(8,128)(2,1)S(1)}, u32[]{:S(2)}, u32[]{:S(2)}) collective-permute-start(bf16[2,512,256]{1,2,0:T(8,128)(2,1)S(1)} %get-tuple-element.635), channel_id=1, source_target_pairs={{0,2},{2,4},{4,6},{6,8},{8,10},{10,12},{12,14},{14,16},{16,18},{18... | collective-permute-start | bytes 1572872 | tf_op jit(solution)/shard_map/while/body/eval_jaxpr/ppermute | solution.py:20
  232.9 21.8 %collective-permute-start.1 = (bf16[2,512,256]{1,2,0:T(8,128)(2,1)S(1)}, bf16[2,512,256]{1,2,0:T(8,128)(2,1)S(1)}, u32[]{:S(2)}, u32[]{:S(2)}) collective-permute-start(bf16[2,512,256]{1,2,0:T(8,128)(2,1)S(1)} %get-tuple-element.636), channel_id=1, source_target_pairs={{2,0},{4,2},{6,4},{8,6},{10,8},{12,10},{14,12},{16,14},{18,16},{20... | collective-permute-start | bytes 1572872 | tf_op jit(solution)/shard_map/while/body/eval_jaxpr/ppermute | solution.py:20
  254.8 8.0 %collective-permute-start = (bf16[2,512,256]{1,2,0:T(8,128)(2,1)S(1)}, bf16[2,512,256]{1,2,0:T(8,128)(2,1)S(1)}, u32[]{:S(2)}, u32[]{:S(2)}) collective-permute-start(bf16[2,512,256]{1,2,0:T(8,128)(2,1)S(1)} %get-tuple-element.635), channel_id=1, source_target_pairs={{0,2},{2,4},{4,6},{6,8},{8,10},{10,12},{12,14},{14,16},{16,18},{18... | collective-permute-start | bytes 1572872 | tf_op jit(solution)/shard_map/while/body/eval_jaxpr/ppermute | solution.py:20
  256.8 26.6 %collective-permute-start.1 = (bf16[2,512,256]{1,2,0:T(8,128)(2,1)S(1)}, bf16[2,512,256]{1,2,0:T(8,128)(2,1)S(1)}, u32[]{:S(2)}, u32[]{:S(2)}) collective-permute-start(bf16[2,512,256]{1,2,0:T(8,128)(2,1)S(1)} %get-tuple-element.636), channel_id=1, source_target_pairs={{2,0},{4,2},{6,4},{8,6},{10,8},{12,10},{14,12},{16,14},{18,16},{20... | collective-permute-start | bytes 1572872 | tf_op jit(solution)/shard_map/while/body/eval_jaxpr/ppermute | solution.py:20
  283.5 8.0 %collective-permute-start = (bf16[2,512,256]{1,2,0:T(8,128)(2,1)S(1)}, bf16[2,512,256]{1,2,0:T(8,128)(2,1)S(1)}, u32[]{:S(2)}, u32[]{:S(2)}) collective-permute-start(bf16[2,512,256]{1,2,0:T(8,128)(2,1)S(1)} %get-tuple-element.635), channel_id=1, source_target_pairs={{0,2},{2,4},{4,6},{6,8},{8,10},{10,12},{12,14},{14,16},{16,18},{18... | collective-permute-start | bytes 1572872 | tf_op jit(solution)/shard_map/while/body/eval_jaxpr/ppermute | solution.py:20
  285.4 27.0 %collective-permute-start.1 = (bf16[2,512,256]{1,2,0:T(8,128)(2,1)S(1)}, bf16[2,512,256]{1,2,0:T(8,128)(2,1)S(1)}, u32[]{:S(2)}, u32[]{:S(2)}) collective-permute-start(bf16[2,512,256]{1,2,0:T(8,128)(2,1)S(1)} %get-tuple-element.636), channel_id=1, source_target_pairs={{2,0},{4,2},{6,4},{8,6},{10,8},{12,10},{14,12},{16,14},{18,16},{20... | collective-permute-start | bytes 1572872 | tf_op jit(solution)/shard_map/while/body/eval_jaxpr/ppermute | solution.py:20
  312.6 8.0 %collective-permute-start = (bf16[2,512,256]{1,2,0:T(8,128)(2,1)S(1)}, bf16[2,512,256]{1,2,0:T(8,128)(2,1)S(1)}, u32[]{:S(2)}, u32[]{:S(2)}) collective-permute-start(bf16[2,512,256]{1,2,0:T(8,128)(2,1)S(1)} %get-tuple-element.635), channel_id=1, source_target_pairs={{0,2},{2,4},{4,6},{6,8},{8,10},{10,12},{12,14},{14,16},{16,18},{18... | collective-permute-start | bytes 1572872 | tf_op jit(solution)/shard_map/while/body/eval_jaxpr/ppermute | solution.py:20
  314.5 27.0 %collective-permute-start.1 = (bf16[2,512,256]{1,2,0:T(8,128)(2,1)S(1)}, bf16[2,512,256]{1,2,0:T(8,128)(2,1)S(1)}, u32[]{:S(2)}, u32[]{:S(2)}) collective-permute-start(bf16[2,512,256]{1,2,0:T(8,128)(2,1)S(1)} %get-tuple-element.636), channel_id=1, source_target_pairs={{2,0},{4,2},{6,4},{8,6},{10,8},{12,10},{14,12},{16,14},{18,16},{20... | collective-permute-start | bytes 1572872 | tf_op jit(solution)/shard_map/while/body/eval_jaxpr/ppermute | solution.py:20
  341.6 8.0 %collective-permute-start = (bf16[2,512,256]{1,2,0:T(8,128)(2,1)S(1)}, bf16[2,512,256]{1,2,0:T(8,128)(2,1)S(1)}, u32[]{:S(2)}, u32[]{:S(2)}) collective-permute-start(bf16[2,512,256]{1,2,0:T(8,128)(2,1)S(1)} %get-tuple-element.635), channel_id=1, source_target_pairs={{0,2},{2,4},{4,6},{6,8},{8,10},{10,12},{12,14},{14,16},{16,18},{18... | collective-permute-start | bytes 1572872 | tf_op jit(solution)/shard_map/while/body/eval_jaxpr/ppermute | solution.py:20
  343.5 25.4 %collective-permute-start.1 = (bf16[2,512,256]{1,2,0:T(8,128)(2,1)S(1)}, bf16[2,512,256]{1,2,0:T(8,128)(2,1)S(1)}, u32[]{:S(2)}, u32[]{:S(2)}) collective-permute-start(bf16[2,512,256]{1,2,0:T(8,128)(2,1)S(1)} %get-tuple-element.636), channel_id=1, source_target_pairs={{2,0},{4,2},{6,4},{8,6},{10,8},{12,10},{14,12},{16,14},{18,16},{20... | collective-permute-start | bytes 1572872 | tf_op jit(solution)/shard_map/while/body/eval_jaxpr/ppermute | solution.py:20
  370.9 20.6 %collective-permute-start.1 = (bf16[2,512,256]{1,2,0:T(8,128)(2,1)S(1)}, bf16[2,512,256]{1,2,0:T(8,128)(2,1)S(1)}, u32[]{:S(2)}, u32[]{:S(2)}) collective-permute-start(bf16[2,512,256]{1,2,0:T(8,128)(2,1)S(1)} %get-tuple-element.636), channel_id=1, source_target_pairs={{2,0},{4,2},{6,4},{8,6},{10,8},{12,10},{14,12},{16,14},{18,16},{20... | collective-permute-start | bytes 1572872 | tf_op jit(solution)/shard_map/while/body/eval_jaxpr/ppermute | solution.py:20
  (7 other events, 773.9 us)
Sparse Core Ops, SparseCore 0:
  401.1 174.5 all-gather.1
where the time goes:
time: 598 us; the launch traced here: 594 us
  waiting for transfers between devices  356 us (60%)
  starting transfers between devices  80.3 us (13%)
  other arithmetic  57.6 us (10%)
  matrix products  43.9 us (7%)
  loops' own time  21.9 us (4%)
  between operations  14.4 us (2%)
  local copies, waits for them, and re-layouts  11.1 us (2%)
  blocking collectives  9.13 us (2%)
    ppermute x32, waiting for transfers between devices, passed_along(): return lax.ppermute(x, axis, pairs)  181 us
    all_gather x1, waiting for transfers between devices, shards(): lax.all_gather(second_cells, ('row', 'col'), axis=0, tiled=True)  175 us
    ppermute x32, starting transfers between devices, passed_along(): return lax.ppermute(x, axis, pairs)  80.3 us
    another operation x1, loops' own time, shards(): lax.fori_loop(0, reach, turn, (state, widened, widened))  21.5 us
    reduce_sum x8, other arithmetic, update(): new_sum = run_sum * rescale + jnp.sum(lifted, axis=-1)  20.5 us
    reduce_or x17, other arithmetic, accumulate(): return lax.cond(jnp.any(allowed), update, lambda state_in: state_in, state)  17.1 us
    dot_general x8, matrix products, update(): jnp.einsum('fhqk,fkhd->fhqd', lifted.astype(jnp.bfloat16), value_part, pr...  16.2 us
    dot_general x8, matrix products, update(): jnp.einsum('fqhd,fkhd->fhqk', queries, key_part, preferred_element_type=j...  13.2 us
  transfers between devices with their start and end apart: 33, of which 32 were waited for; matrix products, arithmetic and copies ran while one was open for 5% of the time, Pallas kernels for 0%

commit v1 on v0

v1 whole, which is shorter than its diff:
```python
import functools
import math

import jax
import jax.numpy as jnp
from jax import lax
from jax.experimental import pallas as pl
from jax.experimental.pallas import tpu as pltpu
from jax.sharding import PartitionSpec as P

HEADS = 8
HEAD_DIM = 16
CHAN = 128
HIDDEN = 1024
NORM_EPSILON = 1e-05
LOG2E = math.log2(math.e)
MESH = pl.DeviceIdType.MESH
F32 = jnp.float32
BF16 = jnp.bfloat16

HALF = 128
TILE = 256
CHUNK = 1024
CORNER, EDGE, OWN, OTHER = 8, 16, 8, 24
UNITS = 18
GROUP = 8


def nn(a, b):
    return jnp.dot(a, b, preferred_element_type=F32)


def nt(a, b):
    return lax.dot_general(a, b, (((1,), (1,)), ((), ())), preferred_element_type=F32)


def layer_norm(values, gain, bias):
    centre = values - jnp.mean(values, axis=-1, keepdims=True)
    spread = jnp.mean(centre * centre, axis=-1, keepdims=True)
    return centre * lax.rsqrt(spread + NORM_EPSILON) * gain + bias


def erf_gelu(x):
    return 0.5 * x * (1.0 + lax.erf(x * (1.0 / math.sqrt(2.0))))


def unit_tile(n):
    tile = jnp.where(n < 4, n, jnp.where(n < 20, 4 + (n - 4) // 2, 12 + (n - 20) // 4))
    chunk = jnp.where(n < 4, 0, jnp.where(n < 20, 1 + lax.rem(n, 2), 3 + lax.rem(n, 4)))
    return tile, chunk


def kernel(
    first, second, attend_w, merge_w, message_gain, message_bias, expand_w, reduce_w, update_gain, update_bias,
    out,
    sent, corner, edge, own, other,
    q_all, k_all, v_all, scores_a, scores_b, max_a, max_b, accs, maxes,
    o_all, attended, ref_q, ref_k, where_v, partial, parts,
    send_sem, corner_sem, edge_sem, own_sem, other_sem,
    back_send_sem, back_sem, ref_send_sem, q_sem, k_sem, part_send_sem, part_sem,
):
    pair, r, c = lax.axis_index("pair"), lax.axis_index("row"), lax.axis_index("col")
    me = r * 2 + c
    side = r // 16
    place = lax.rem(r, 16)
    head, frame = place // 2, lax.rem(place, 2)
    middle = (r >= 8) & (r < 24)

    barrier = pltpu.get_barrier_semaphore()

    def greet(i, carry):
        peer = lax.rem(me + 1 + i, 64)
        pl.semaphore_signal(barrier, inc=1, device_id=(pair, peer // 2, lax.rem(peer, 2)), device_id_type=MESH)
        return carry

    lax.fori_loop(0, 63, greet, 0)

    weight_t = attend_w[...].T
    for f, source in enumerate((first, second)):
        for half in range(2):
            cells = source[:, 32 * half : 32 * half + 32, :].reshape(HALF, CHAN)
            projected = nt(weight_t, cells)
            queries = projected[:CHAN] * (LOG2E / math.sqrt(HEAD_DIM))
            sent[f, half, :, 0:16, :] = queries.astype(BF16).reshape(HEADS, 16, HALF)
            sent[f, half, :, 16:32, :] = projected[CHAN : 2 * CHAN].astype(BF16).reshape(HEADS, 16, HALF)
            sent[f, half, :, 32:48, :] = projected[2 * CHAN :].astype(BF16).reshape(HEADS, 16, HALF)

    pl.semaphore_wait(barrier, 63)

    def transfer(source, target, dest_r, dest_c, s_sem, r_sem, start):
        here = (dest_r == r) & (dest_c == c)

        @pl.when(jnp.logical_not(here))
        def _():
            copy = pltpu.make_async_remote_copy(
                source, target, s_sem, r_sem, device_id=(pair, dest_r, dest_c), device_id_type=MESH
            )
            if start:
                copy.start()
            else:
                copy.wait_send()

        if start:

            @pl.when(here)
            def _():
                pltpu.make_async_copy(source, target, r_sem).start()

    def send_all(start):
        def each(body):
            def step(i, carry):
                d = lax.rem(place + i, 16)
                body(d // 2, lax.rem(d, 2), d)
                return carry

            lax.fori_loop(0, 16, step, 0)

        inner = 1 - c

        @pl.when(middle)
        def _():
            def outer_half(h, f, d):
                transfer(sent.at[f, c, h], edge.at[r - 8], (1 - c) * 16 + d, c, send_sem, edge_sem, start)

            def own_half(h, f, d):
                transfer(sent.at[f, inner, h], own.at[lax.rem(r, 8)], side * 16 + d, c, send_sem, own_sem, start)

            def other_halves(h, f, d):
                for turn in range(1, 4):
                    to_side, to_c = side ^ (turn // 2), c ^ (turn % 2)
                    transfer(
                        sent.at[f, inner, h, 16:48],
                        other.at[(turn - 1) * 8 + lax.rem(r, 8)],
                        to_side * 16 + d, to_c, send_sem, other_sem, start,
                    )

            each(outer_half)
            each(own_half)
            each(other_halves)

        @pl.when(jnp.logical_not(middle))
        def _():
            def corner_half(h, f, d):
                transfer(sent.at[f, c, h], corner.at[lax.rem(r, 8)], side * 16 + d, c, send_sem, corner_sem, start)

            def edge_half(h, f, d):
                slot = c * 8 + lax.rem(r, 8)
                transfer(sent.at[f, inner, h], edge.at[slot], side * 16 + d, side, send_sem, edge_sem, start)

            each(corner_half)
            each(edge_half)

    send_all(True)

    def arrived(ref, sem):
        pltpu.make_async_copy(ref, ref, sem).wait()

    def take_kv(block, at, first_row):
        k_all[at * HALF : (at + 1) * HALF, :] = block[first_row : first_row + 16, :].astype(F32).T.astype(BF16)
        v_all[0:16, at * HALF : (at + 1) * HALF] = block[first_row + 16 : first_row + 32, :]

    def take_q(block, at):
        q_all[at // 2, :, (at % 2) * HALF : (at % 2 + 1) * HALF] = block[0:16, :]

    v_all[16:32, :] = jnp.ones_like(v_all[16:32, :])
    arrived(corner, corner_sem)
    for b in range(CORNER):
        take_kv(corner[b], b, 16)
        take_q(corner[b], b)
    arrived(edge, edge_sem)
    for b in range(EDGE):
        take_kv(edge[b], 8 + b, 16)
        take_q(edge[b], 8 + b)

    def score_pass(u, scores, top):
        for sub in range(2):
            tile, chunk = unit_tile(2 * u + sub)
            keys = k_all[pl.ds(pl.multiple_of(chunk * CHUNK, CHUNK), CHUNK), :]
            x = nn(keys, q_all[tile])
            scores[sub * CHUNK : (sub + 1) * CHUNK, :] = x
            top[sub] = jnp.max(x.reshape(CHUNK // 8, 8, TILE), axis=0)

    def value_pass(u, scores, top):
        for sub in range(2):
            n = 2 * u + sub
            _, chunk = unit_tile(n)
            values = v_all[:, pl.ds(pl.multiple_of(chunk * CHUNK, CHUNK), CHUNK)]
            m = jnp.max(top[sub], axis=0, keepdims=True)
            p = jnp.exp2(scores[sub * CHUNK : (sub + 1) * CHUNK, :] - m).astype(BF16)
            accs[n] = nn(values, p)
            maxes[n] = jnp.broadcast_to(m, (8, TILE))

    def finish(tile, n, count):
        m = maxes[n, 0:1]
        for j in range(1, count):
            m = jnp.maximum(m, maxes[n + j, 0:1])
        acc = accs[n] * jnp.exp2(maxes[n, 0:1] - m)
        for j in range(1, count):
            acc = acc + accs[n + j] * jnp.exp2(maxes[n + j, 0:1] - m)
        o = (acc[0:16] / acc[16:17]).astype(BF16)
        o_all[2 * tile] = o[:, :HALF]
        o_all[2 * tile + 1] = o[:, HALF:]

    def give_back(kind, start):
        def step(j, carry):
            if kind == "corner":
                at, to_r, to_c, half = j, side * 24 + j, c, c
            elif kind == "edge":
                level = side == c
                at = CORNER + j
                to_r = jnp.where(level, side * 24 + lax.rem(j, 8), 8 + j)
                to_c = jnp.where(level, j // 8, c)
                half = jnp.where(level, 1 - to_c, to_c)
            else:
                at, to_r, to_c, half = CORNER + EDGE + j, 8 + 8 * side + j, c, 1 - c
            transfer(o_all.at[at], attended.at[frame, half, head], to_r, to_c, back_send_sem, back_sem, start)
            return carry

        lax.fori_loop(0, EDGE if kind == "edge" else 8, step, 0)

    score_pass(0, scores_a, max_a)

    def two_units(i, carry):
        @pl.when(i == 4)
        def _():
            arrived(own, own_sem)
            for b in range(OWN):
                take_kv(own[b], 24 + b, 16)
                take_q(own[b], 24 + b)
            arrived(other, other_sem)
            for b in range(OTHER):
                take_kv(other[b], 32 + b, 0)

        @pl.when(i == 5)
        def _():
            for tile in range(4):
                finish(tile, tile, 1)
            give_back("corner", True)
            for tile in range(8):
                finish(4 + tile, 4 + 2 * tile, 2)
            give_back("edge", True)

        score_pass(2 * i + 1, scores_b, max_b)
        value_pass(2 * i, scores_a, max_a)
        score_pass(jnp.minimum(2 * i + 2, UNITS - 1), scores_a, max_a)
        value_pass(2 * i + 1, scores_b, max_b)
        return carry

    lax.fori_loop(0, UNITS // 2, two_units, 0)
    for tile in range(4):
        finish(12 + tile, 20 + 4 * tile, 4)
    give_back("centre", True)

    send_all(False)
    for kind in ("corner", "edge", "centre"):
        give_back(kind, False)
    arrived(attended, back_sem)

    def refine(f, source):
        cells = jnp.concatenate(
            [source[:, 32 * half : 32 * half + 32, :].reshape(HALF, CHAN) for half in range(2)], axis=0
        )
        heads = jnp.concatenate(
            [attended[f, half].reshape(CHAN, HALF).astype(F32).T.astype(BF16) for half in range(2)], axis=0
        )
        message = layer_norm(nn(heads, merge_w[...]), message_gain[...], message_bias[...]).astype(BF16)
        joined = jnp.concatenate([cells, message], axis=1)
        update = jnp.zeros((2 * HALF, CHAN), F32)
        for j in range(HIDDEN // 256):
            hidden = erf_gelu(nn(joined, expand_w[:, 256 * j : 256 * j + 256])).astype(BF16)
            update = update + nn(hidden, reduce_w[256 * j : 256 * j + 256, :])
        return cells.astype(F32) + layer_norm(update, update_gain[...], update_bias[...])

    column, line = lax.rem(r, 8), r // 8

    def spread(kind, start):
        def step(i, carry):
            if kind == "k":
                to = lax.rem(line * 2 + c + i, GROUP)
                to_r, to_c, at, ref, sem = (to // 2) * 8 + column, lax.rem(to, 2), line * 2 + c, ref_k, k_sem
            else:
                to_r, to_c, at, ref, sem = line * 8 + lax.rem(column + i, GROUP), c, column, ref_q, q_sem
            copy = pltpu.make_async_remote_copy(
                ref.at[at], ref.at[at], ref_send_sem, sem, device_id=(pair, to_r, to_c), device_id_type=MESH
            )
            if start:
                copy.start()
            else:
                copy.wait_send()
            return carry

        lax.fori_loop(1, GROUP, step, 0)

    ref_k[line * 2 + c] = refine(1, second).astype(BF16)
    spread("k", True)
    ref_q[column] = (refine(0, first) * (LOG2E / math.sqrt(CHAN))).astype(BF16)
    spread("q", True)

    at = lax.broadcasted_iota(jnp.int32, (16, TILE), 1)
    what = lax.broadcasted_iota(jnp.int32, (16, TILE), 0)
    for k in range(GROUP):
        key_column = 64 * (k % 2) + 32 * (at // HALF) + at % 32
        key_row = 4 * (8 * (k // 2) + column) + (at // 32) % 4
        weigh = jnp.where(what == 0, 1, jnp.where(what == 1, key_column, key_row))
        where_v[:, TILE * k : TILE * (k + 1)] = weigh.astype(F32).astype(BF16)

    pltpu.make_async_copy(ref_k.at[0:7], ref_k.at[0:7], k_sem).wait()
    pltpu.make_async_copy(ref_q.at[0:7], ref_q.at[0:7], q_sem).wait()

    def corr_scores(t, scores, top):
        x = nt(ref_k[...].reshape(GROUP * TILE, CHAN), ref_q[t])
        scores[...] = x
        top[0] = jnp.max(x.reshape(GROUP * TILE // 8, 8, TILE), axis=0)

    def corr_sums(t, scores, top):
        m = jnp.max(top[0], axis=0, keepdims=True)
        p = jnp.exp2(scores[...] - m).astype(BF16)
        sums = nn(where_v[...], p)
        partial[t] = jnp.concatenate([sums[0:7], m], axis=0)

    corr_scores(0, scores_a, max_a)

    def two_tiles(i, carry):
        corr_scores(2 * i + 1, scores_b, max_b)
        corr_sums(2 * i, scores_a, max_a)
        corr_scores(jnp.minimum(2 * i + 2, GROUP - 1), scores_a, max_a)
        corr_sums(2 * i + 1, scores_b, max_b)
        return carry

    lax.fori_loop(0, GROUP // 2, two_tiles, 0)

    def hand_in(start):
        def step(i, carry):
            to = lax.rem(column + i, GROUP)
            copy = pltpu.make_async_remote_copy(
                partial.at[to], parts.at[column], part_send_sem, part_sem,
                device_id=(pair, line * 8 + to, c), device_id_type=MESH,
            )
            if start:
                copy.start()
            else:
                copy.wait_send()
            return carry

        lax.fori_loop(1, GROUP, step, 0)

    hand_in(True)
    parts[column] = partial[column]
    spread("k", False)
    spread("q", False)
    hand_in(False)
    pltpu.make_async_copy(parts.at[0:7], parts.at[0:7], part_sem).wait()

    m = jnp.max(parts[:, 7:8, :], axis=0)
    total = jnp.zeros((8, TILE), F32)
    for j in range(GROUP):
        total = total + parts[j] * jnp.exp2(parts[j, 7:8, :] - m)
    lane = lax.broadcasted_iota(jnp.int32, (1, TILE), 1)
    own_column = (64 * c + 32 * (lane // HALF) + lane % 32).astype(F32)
    own_row = (4 * r + (lane // 32) % 4).astype(F32)
    flows = (
        (total[1:2] / total[0:1] - own_column) * (2.0 / 128),
        (total[2:3] / total[0:1] - own_row) * (2.0 / 128),
    )
    for which in range(2):
        for i in range(4):
            for half in range(2):
                start = half * HALF + 32 * i
                out[which, i : i + 1, 32 * half : 32 * half + 32] = flows[which][:, start : start + 32]


def shards(first, second, attend_w, merge_w, message_gain, message_bias, expand_w, reduce_w, update_gain, update_bias):
    rows = [v.reshape(1, CHAN) for v in (message_gain, message_bias, update_gain, update_bias)]
    vmem = pl.BlockSpec(memory_space=pltpu.VMEM)
    dma = pltpu.SemaphoreType.DMA
    return pl.pallas_call(
        kernel,
        out_shape=jax.ShapeDtypeStruct((2, 4, 64), F32),
        in_specs=[vmem] * 10,
        out_specs=vmem,
        scratch_shapes=[
            pltpu.VMEM((2, 2, HEADS, 48, HALF), BF16),
            pltpu.VMEM((CORNER, 48, HALF), BF16),
            pltpu.VMEM((EDGE, 48, HALF), BF16),
            pltpu.VMEM((OWN, 48, HALF), BF16),
            pltpu.VMEM((OTHER, 32, HALF), BF16),
            pltpu.VMEM((16, 16, TILE), BF16),
            pltpu.VMEM((7 * CHUNK, 16), BF16),
            pltpu.VMEM((32, 7 * CHUNK), BF16),
            pltpu.VMEM((2 * CHUNK, TILE), F32),
            pltpu.VMEM((2 * CHUNK, TILE), F32),
            pltpu.VMEM((2, 8, TILE), F32),
            pltpu.VMEM((2, 8, TILE), F32),
            pltpu.VMEM((2 * UNITS, 32, TILE), F32),
            pltpu.VMEM((2 * UNITS, 8, TILE), F32),
            pltpu.VMEM((32, 16, HALF), BF16),
            pltpu.VMEM((2, 2, HEADS, 16, HALF), BF16),
            pltpu.VMEM((GROUP, TILE, CHAN), BF16),
            pltpu.VMEM((GROUP, TILE, CHAN), BF16),
            pltpu.VMEM((16, GROUP * TILE), BF16),
            pltpu.VMEM((GROUP, 8, TILE), F32),
            pltpu.VMEM((GROUP, 8, TILE), F32),
        ]
        + [dma] * 12,
        compiler_params=pltpu.CompilerParams(
            collective_id=0, has_side_effects=True, vmem_limit_bytes=40 * 1024 * 1024
        ),
    )(first, second, attend_w, merge_w, rows[0], rows[1], expand_w, reduce_w, rows[2], rows[3])


def solution(mesh):
    split = P(("pair", "row"), "col", None)
    return jax.shard_map(
        shards,
        mesh=mesh,
        in_specs=(split, split) + (P(),) * 8,
        out_specs=P(None, ("pair", "row"), "col"),
        check_vma=False,
    )
```

time: 598 us -> 56.5 us (0.09)
  waiting for transfers between devices: 356 us -> 0 us
  starting transfers between devices: 80.3 us -> 0 us
  other arithmetic: 57.6 us -> 0 us
  Pallas kernels: 0 us -> 49.4 us
  matrix products: 43.9 us -> 0 us
  loops' own time: 21.9 us -> 0 us
  between operations: 14.4 us -> 0.03 us
  blocking collectives: 9.13 us -> 0 us
    ppermute x32 -> x0, waiting for transfers between devices: 181 us -> none  [passed_along(): return lax.ppermute(x, axis, pairs)]
    all_gather x1 -> x0, waiting for transfers between devices: 175 us -> none  [shards(): lax.all_gather(second_cells, ('row', 'col'), axis=0, tiled=True)]
    ppermute x32 -> x0, starting transfers between devices: 80.3 us -> none  [passed_along(): return lax.ppermute(x, axis, pairs)]
    pallas_call x0 -> x1, Pallas kernels: none -> 49.4 us  [shards(): pl.pallas_call(kernel, out_shape=jax.ShapeDtypeStruct((2, 4, 64), F32), i...]
    dot_general x22 -> x0, matrix products: 43.9 us -> none  [the longest x8 16.2 us: update(): jnp.einsum('fhqk,fkhd->fhqd', lifted.astype(jnp.bfloat16), value_part, pr...]
    reduce_sum x11 -> x0, other arithmetic: 26.4 us -> none  [the longest x8 20.5 us: update(): new_sum = run_sum * rescale + jnp.sum(lifted, axis=-1)]
    another operation x34 -> x0, loops' own time: 21.9 us -> none  [the longest x1 21.5 us: shards(): lax.fori_loop(0, reach, turn, (state, widened, widened))]
    reduce_or x17 -> x0, other arithmetic: 17.1 us -> none  [accumulate(): return lax.cond(jnp.any(allowed), update, lambda state_in: state_in, state)]
  transfers between devices with their start and end apart: 33 -> 0, of which waited for: 32 -> 0; matrix products, arithmetic and copies ran while one was open for 5% -> 0% of each run, Pallas kernels for 0% -> 0%
where the time goes in v1:
time: 56.5 us; the launch traced here: 56.1 us
  Pallas kernels  49.4 us (87%)
  local copies, waits for them, and re-layouts  6.6 us (12%)
    pallas_call x1, Pallas kernels, shards(): pl.pallas_call(kernel, out_shape=jax.ShapeDtypeStruct((2, 4, 64), F32), i...  49.4 us
    unnamed x21, local copies, waits for them, and re-layouts  6.6 us

profile of v1, /device:TPU:1, one launch (start us, length us, event | category | flops | bytes accessed | tf_op | source)
XLA Modules:
  0.0 56.1 jit_solution(10891751455499658732)
XLA Ops:
  0.0 0.0 copy-start.9
  0.0 0.0 copy-start.6
  0.0 0.0 copy-start.7
  0.0 0.0 copy-start.8
  0.0 0.6 %copy-done.9 = f32[128]{0:T(128)S(1)} copy-done((f32[128]{0:T(128)S(1)}, f32[128]{0:T(128)}, u32[]{:S(2)}) %copy-start.9) | copy-done | bytes 536
  0.7 0.0 copy-done.6
  0.7 0.0 copy-done.7
  0.7 0.0 copy-done.8
  0.7 0.0 copy-start
  0.7 1.0 %copy-done = bf16[256,1024]{1,0:T(8,128)(2,1)S(1)} copy-done((bf16[256,1024]{1,0:T(8,128)(2,1)S(1)}, bf16[256,1024]{1,0:T(8,128)(2,1)}, u32[]{:S(2)}) %copy-start) | copy-done | bytes 524312
  1.7 0.0 copy-start.1
  1.7 0.9 %copy-done.1 = bf16[1024,128]{1,0:T(8,128)(2,1)S(1)} copy-done((bf16[1024,128]{1,0:T(8,128)(2,1)S(1)}, bf16[1024,128]{1,0:T(8,128)(2,1)}, u32[]{:S(2)}) %copy-start.1) | copy-done | bytes 262168
  2.7 0.0 copy-start.2
  2.7 0.9 %copy-done.2 = bf16[128,384]{1,0:T(8,128)(2,1)S(1)} copy-done((bf16[128,384]{1,0:T(8,128)(2,1)S(1)}, bf16[128,384]{1,0:T(8,128)(2,1)}, u32[]{:S(2)}) %copy-start.2) | copy-done | bytes 98328
  3.6 0.0 copy-start.3
  3.6 0.8 %copy-done.3 = bf16[4,64,128]{2,1,0:T(8,128)(2,1)S(1)} copy-done((bf16[4,64,128]{2,1,0:T(8,128)(2,1)S(1)}, bf16[4,64,128]{2,1,0:T(8,128)(2,1)}, u32[]{:S(2)}) %copy-start.3) | copy-done | bytes 65560
  4.4 0.0 copy-start.4
  4.4 0.8 %copy-done.4 = bf16[4,64,128]{2,1,0:T(8,128)(2,1)S(1)} copy-done((bf16[4,64,128]{2,1,0:T(8,128)(2,1)S(1)}, bf16[4,64,128]{2,1,0:T(8,128)(2,1)}, u32[]{:S(2)}) %copy-start.4) | copy-done | bytes 65560
  5.3 0.0 copy-start.5
  5.3 0.8 %copy-done.5 = bf16[128,128]{1,0:T(8,128)(2,1)S(1)} copy-done((bf16[128,128]{1,0:T(8,128)(2,1)S(1)}, bf16[128,128]{1,0:T(8,128)(2,1)}, u32[]{:S(2)}) %copy-start.5) | copy-done | bytes 32792
  6.0 49.4 %shard_map.100 = f32[2,4,64]{2,1,0:T(4,128)S(1)} custom-call(bf16[4,64,128]{2,1,0:T(8,128)(2,1)S(1)} %copy-done.3, bf16[4,64,128]{2,1,0:T(8,128)(2,1)S(1)} %copy-done.4, bf16[128,384]{1,0:T(8,128)(2,1)S(1)} %copy-done.2, bf16[128,128]{1,0:T(8,128)(2,1)S(1)} %copy-done.5, f32[1,128]{1,0:T(1,128)S(1)} %bitcast.4, f32[1,128]{1,0:T(1,128)S(1)} %bitcast.5, ...), custom_call_target="tpu_custom_call" | custom-call | tf_op jit(solution)/shard_map/pallas_call | solution.py:376
  55.5 0.6 %copy.12 = f32[2,4,64]{2,1,0:T(4,128)} copy(f32[2,4,64]{2,1,0:T(4,128)S(1)} %shard_map.100) | data formatting | bytes 4096
Async XLA Ops:
  0.0 0.7 %copy-start.9 = (f32[128]{0:T(128)S(1)}, f32[128]{0:T(128)}, u32[]{:S(2)}) copy-start(f32[128]{0:T(128)} %param.19) | copy-start | bytes 1540
  0.0 0.7 %copy-start.6 = (f32[128]{0:T(128)S(1)}, f32[128]{0:T(128)}, u32[]{:S(2)}) copy-start(f32[128]{0:T(128)} %param.14) | copy-start | bytes 1540
  0.0 0.7 %copy-start.7 = (f32[128]{0:T(128)S(1)}, f32[128]{0:T(128)}, u32[]{:S(2)}) copy-start(f32[128]{0:T(128)} %param.15) | copy-start | bytes 1540
  0.0 0.7 %copy-start.8 = (f32[128]{0:T(128)S(1)}, f32[128]{0:T(128)}, u32[]{:S(2)}) copy-start(f32[128]{0:T(128)} %param.18) | copy-start | bytes 1540
  0.7 1.0 %copy-start = (bf16[256,1024]{1,0:T(8,128)(2,1)S(1)}, bf16[256,1024]{1,0:T(8,128)(2,1)}, u32[]{:S(2)}) copy-start(bf16[256,1024]{1,0:T(8,128)(2,1)} %expand_w.1) | copy-start | bytes 1572868
  1.7 0.9 %copy-start.1 = (bf16[1024,128]{1,0:T(8,128)(2,1)S(1)}, bf16[1024,128]{1,0:T(8,128)(2,1)}, u32[]{:S(2)}) copy-start(bf16[1024,128]{1,0:T(8,128)(2,1)} %reduce_w.1) | copy-start | bytes 786436
  2.7 0.9 %copy-start.2 = (bf16[128,384]{1,0:T(8,128)(2,1)S(1)}, bf16[128,384]{1,0:T(8,128)(2,1)}, u32[]{:S(2)}) copy-start(bf16[128,384]{1,0:T(8,128)(2,1)} %attend_w.1) | copy-start | bytes 294916
  3.6 0.8 %copy-start.3 = (bf16[4,64,128]{2,1,0:T(8,128)(2,1)S(1)}, bf16[4,64,128]{2,1,0:T(8,128)(2,1)}, u32[]{:S(2)}) copy-start(bf16[4,64,128]{2,1,0:T(8,128)(2,1)} %first.1) | copy-start | bytes 196612
  4.4 0.8 %copy-start.4 = (bf16[4,64,128]{2,1,0:T(8,128)(2,1)S(1)}, bf16[4,64,128]{2,1,0:T(8,128)(2,1)}, u32[]{:S(2)}) copy-start(bf16[4,64,128]{2,1,0:T(8,128)(2,1)} %second.1) | copy-start | bytes 196612
  5.3 0.8 %copy-start.5 = (bf16[128,128]{1,0:T(8,128)(2,1)S(1)}, bf16[128,128]{1,0:T(8,128)(2,1)}, u32[]{:S(2)}) copy-start(bf16[128,128]{1,0:T(8,128)(2,1)} %merge_w.1) | copy-start | bytes 98308

commit v2 on v1

--- a/solution.py
+++ b/solution.py
@@ -19,10 +19,12 @@
 BF16 = jnp.bfloat16
 
 HALF = 128
-TILE = 256
+TILE = 512
 CHUNK = 1024
+PIECE = 256
+CELLS = 256
 CORNER, EDGE, OWN, OTHER = 8, 16, 8, 24
-UNITS = 18
+UNITS = 9
 GROUP = 8
 
 
@@ -45,20 +47,24 @@
 
 
 def unit_tile(n):
-    tile = jnp.where(n < 4, n, jnp.where(n < 20, 4 + (n - 4) // 2, 12 + (n - 20) // 4))
-    chunk = jnp.where(n < 4, 0, jnp.where(n < 20, 1 + lax.rem(n, 2), 3 + lax.rem(n, 4)))
+    tile = jnp.where(n < 2, n, jnp.where(n < 10, 2 + (n - 2) // 2, 6 + (n - 10) // 4))
+    chunk = jnp.where(n < 2, 0, jnp.where(n < 10, 1 + lax.rem(n, 2), 3 + lax.rem(n - 10, 4)))
     return tile, chunk
 
 
-def kernel(
-    first, second, attend_w, merge_w, message_gain, message_bias, expand_w, reduce_w, update_gain, update_bias,
-    out,
+def kernel(*refs):
+    inputs, out, held, refs = refs[:10], refs[10], refs[11:21], refs[21:]
+    (first, second, attend_w, merge_w, message_gain, message_bias, expand_w, reduce_w, update_gain, update_bias) = held
+    (
     sent, corner, edge, own, other,
     q_all, k_all, v_all, scores_a, scores_b, max_a, max_b, accs, maxes,
     o_all, attended, ref_q, ref_k, where_v, partial, parts,
     send_sem, corner_sem, edge_sem, own_sem, other_sem,
-    back_send_sem, back_sem, ref_send_sem, q_sem, k_sem, part_send_sem, part_sem,
-):
+    back_send_sem, back_sem, ref_send_sem, q_sem, k_sem, part_send_sem, part_sem, k_far_sem, load_sem,
+    ) = refs
+    loads = [pltpu.make_async_copy(inputs[j], held[j], load_sem.at[j]) for j in range(10)]
+    for j in (0, 1, 2, 3, 4, 5, 6, 7, 8, 9):
+        loads[j].start()
     pair, r, c = lax.axis_index("pair"), lax.axis_index("row"), lax.axis_index("col")
     me = r * 2 + c
     side = r // 16
@@ -74,6 +80,9 @@
         return carry
 
     lax.fori_loop(0, 63, greet, 0)
+
+    for j in (0, 1, 2):
+        loads[j].wait()
 
     weight_t = attend_w[...].T
     for f, source in enumerate((first, second)):
@@ -160,35 +169,66 @@
         v_all[0:16, at * HALF : (at + 1) * HALF] = block[first_row + 16 : first_row + 32, :]
 
     def take_q(block, at):
-        q_all[at // 2, :, (at % 2) * HALF : (at % 2 + 1) * HALF] = block[0:16, :]
+        q_all[at // 4, :, (at % 4) * HALF : (at % 4 + 1) * HALF] = block[0:16, :]
+
+    def together(score, value):
+        for sub in range(2):
+            if score:
+                scores, top, get_queries, get_keys = score
+                queries = get_queries(sub)
+                largest = jnp.full((8, TILE), -jnp.inf, F32)
+            if value:
+                lifted, tops, get_values, put = value
+                m = jnp.max(tops[sub], axis=0, keepdims=True)
+                acc = None
+            for j in range(CHUNK // PIECE):
+                at = slice(sub * CHUNK + j * PIECE, sub * CHUNK + (j + 1) * PIECE)
+                if score:
+                    x = get_keys(sub, j, queries)
+                    scores[at, :] = x
+                    largest = jnp.maximum(largest, jnp.max(x.reshape(PIECE // 8, 8, TILE), axis=0))
+                if value:
+                    p = jnp.exp2(lifted[at, :] - m).astype(BF16)
+                    product = nn(get_values(sub, j), p)
+                    acc = product if acc is None else acc + product
+            if score:
+                top[sub] = largest
+            if value:
+                put(sub, m, acc)
+
+    held_scores = ((scores_a, max_a), (scores_b, max_b))
+
+    def attend_score(u, slot):
+        def get_queries(sub):
+            return q_all[unit_tile(2 * u + sub)[0]]
+
+        def get_scores(sub, j, queries):
+            first_key = unit_tile(2 * u + sub)[1] * CHUNK + j * PIECE
+            return nn(k_all[pl.ds(pl.multiple_of(first_key, PIECE), PIECE), :], queries)
+
+        return (*held_scores[slot], get_queries, get_scores)
+
+    def attend_value(u, slot):
+        def get_values(sub, j):
+            first_key = unit_tile(2 * u + sub)[1] * CHUNK + j * PIECE
+            return v_all[:, pl.ds(pl.multiple_of(first_key, PIECE), PIECE)]
+
+        def put(sub, m, acc):
+            accs[2 * u + sub] = acc
+            maxes[2 * u + sub] = jnp.broadcast_to(m, (8, TILE))
+
+        return (*held_scores[slot], get_values, put)
 
     v_all[16:32, :] = jnp.ones_like(v_all[16:32, :])
     arrived(corner, corner_sem)
     for b in range(CORNER):
         take_kv(corner[b], b, 16)
         take_q(corner[b], b)
+    together(attend_score(0, 0), None)
     arrived(edge, edge_sem)
     for b in range(EDGE):
         take_kv(edge[b], 8 + b, 16)
         take_q(edge[b], 8 + b)
-
-    def score_pass(u, scores, top):
-        for sub in range(2):
-            tile, chunk = unit_tile(2 * u + sub)
-            keys = k_all[pl.ds(pl.multiple_of(chunk * CHUNK, CHUNK), CHUNK), :]
-            x = nn(keys, q_all[tile])
-            scores[sub * CHUNK : (sub + 1) * CHUNK, :] = x
-            top[sub] = jnp.max(x.reshape(CHUNK // 8, 8, TILE), axis=0)
-
-    def value_pass(u, scores, top):
-        for sub in range(2):
-            n = 2 * u + sub
-            _, chunk = unit_tile(n)
-            values = v_all[:, pl.ds(pl.multiple_of(chunk * CHUNK, CHUNK), CHUNK)]
-            m = jnp.max(top[sub], axis=0, keepdims=True)
-            p = jnp.exp2(scores[sub * CHUNK : (sub + 1) * CHUNK, :] - m).astype(BF16)
-            accs[n] = nn(values, p)
-            maxes[n] = jnp.broadcast_to(m, (8, TILE))
 
     def finish(tile, n, count):
         m = maxes[n, 0:1]
@@ -198,8 +238,8 @@
         for j in range(1, count):
             acc = acc + accs[n + j] * jnp.exp2(maxes[n + j, 0:1] - m)
         o = (acc[0:16] / acc[16:17]).astype(BF16)
-        o_all[2 * tile] = o[:, :HALF]
-        o_all[2 * tile + 1] = o[:, HALF:]
+        for b in range(4):
+            o_all[4 * tile + b] = o[:, b * HALF : (b + 1) * HALF]
 
     def give_back(kind, start):
         def step(j, carry):
@@ -218,10 +258,8 @@
 
         lax.fori_loop(0, EDGE if kind == "edge" else 8, step, 0)
 
-    score_pass(0, scores_a, max_a)
-
     def two_units(i, carry):
-        @pl.when(i == 4)
+        @pl.when(i == 2)
         def _():
             arrived(own, own_sem)
             for b in range(OWN):
@@ -231,30 +269,32 @@
             for b in range(OTHER):
                 take_kv(other[b], 32 + b, 0)
 
-        @pl.when(i == 5)
+        together(attend_score(2 * i + 1, 1), attend_value(2 * i, 0))
+
+        @pl.when(i == 2)
         def _():
-            for tile in range(4):
+            for tile in range(2):
                 finish(tile, tile, 1)
             give_back("corner", True)
-            for tile in range(8):
-                finish(4 + tile, 4 + 2 * tile, 2)
+            for tile in range(4):
+                finish(2 + tile, 2 + 2 * tile, 2)
             give_back("edge", True)
 
-        score_pass(2 * i + 1, scores_b, max_b)
-        value_pass(2 * i, scores_a, max_a)
-        score_pass(jnp.minimum(2 * i + 2, UNITS - 1), scores_a, max_a)
-        value_pass(2 * i + 1, scores_b, max_b)
+        together(attend_score(2 * i + 2, 0), attend_value(2 * i + 1, 1))
         return carry
 
     lax.fori_loop(0, UNITS // 2, two_units, 0)
-    for tile in range(4):
-        finish(12 + tile, 20 + 4 * tile, 4)
+    together(None, attend_value(UNITS - 1, 0))
+    for tile in range(2):
+        finish(6 + tile, 10 + 4 * tile, 4)
     give_back("centre", True)
 
     send_all(False)
     for kind in ("corner", "edge", "centre"):
         give_back(kind, False)
     arrived(attended, back_sem)
+    for j in range(3, 10):
+        loads[j].wait()
 
     def refine(f, source):
         cells = jnp.concatenate(
@@ -276,86 +316,119 @@
     def spread(kind, start):
         def step(i, carry):
             if kind == "k":
-                to = lax.rem(line * 2 + c + i, GROUP)
-                to_r, to_c, at, ref, sem = (to // 2) * 8 + column, lax.rem(to, 2), line * 2 + c, ref_k, k_sem
+                to_line, to_c = lax.rem(line + i // 2, 4), c ^ lax.rem(i, 2)
+                at = lax.rem(4 - i // 2, 4) * 2 + lax.rem(i, 2)
+                for near in (True, False):
+
+                    @pl.when((at < 4) == near)
+                    def _():
+                        copy = pltpu.make_async_remote_copy(
+                            ref_k.at[0], ref_k.at[at], ref_send_sem, k_sem if near else k_far_sem,
+                            device_id=(pair, to_line * 8 + column, to_c), device_id_type=MESH,
+                        )
+                        if start:
+                            copy.start()
+                        else:
+                            copy.wait_send()
             else:
-                to_r, to_c, at, ref, sem = line * 8 + lax.rem(column + i, GROUP), c, column, ref_q, q_sem
-            copy = pltpu.make_async_remote_copy(
-                ref.at[at], ref.at[at], ref_send_sem, sem, device_id=(pair, to_r, to_c), device_id_type=MESH
-            )
-            if start:
-                copy.start()
-            else:
-                copy.wait_send()
+                copy = pltpu.make_async_remote_copy(
+                    ref_q.at[column], ref_q.at[column], ref_send_sem, q_sem,
+                    device_id=(pair, line * 8 + lax.rem(column + i, GROUP), c), device_id_type=MESH,
+                )
+                if start:
+                    copy.start()
+                else:
+                    copy.wait_send()
             return carry
 
         lax.fori_loop(1, GROUP, step, 0)
 
-    ref_k[line * 2 + c] = refine(1, second).astype(BF16)
+    ref_k[0] = refine(1, second).astype(BF16)
     spread("k", True)
     ref_q[column] = (refine(0, first) * (LOG2E / math.sqrt(CHAN))).astype(BF16)
     spread("q", True)
 
-    at = lax.broadcasted_iota(jnp.int32, (16, TILE), 1)
-    what = lax.broadcasted_iota(jnp.int32, (16, TILE), 0)
+    at = lax.broadcasted_iota(jnp.int32, (16, CELLS), 1)
+    what = lax.broadcasted_iota(jnp.int32, (16, CELLS), 0)
     for k in range(GROUP):
-        key_column = 64 * (k % 2) + 32 * (at // HALF) + at % 32
-        key_row = 4 * (8 * (k // 2) + column) + (at // 32) % 4
+        key_column = 64 * (c ^ (k % 2)) + 32 * (at // HALF) + at % 32
+        key_row = 4 * (8 * lax.rem(line + k // 2, 4) + column) + (at // 32) % 4
         weigh = jnp.where(what == 0, 1, jnp.where(what == 1, key_column, key_row))
-        where_v[:, TILE * k : TILE * (k + 1)] = weigh.astype(F32).astype(BF16)
-
-    pltpu.make_async_copy(ref_k.at[0:7], ref_k.at[0:7], k_sem).wait()
-    pltpu.make_async_copy(ref_q.at[0:7], ref_q.at[0:7], q_sem).wait()
-
-    def corr_scores(t, scores, top):
-        x = nt(ref_k[...].reshape(GROUP * TILE, CHAN), ref_q[t])
-        scores[...] = x
-        top[0] = jnp.max(x.reshape(GROUP * TILE // 8, 8, TILE), axis=0)
-
-    def corr_sums(t, scores, top):
-        m = jnp.max(top[0], axis=0, keepdims=True)
-        p = jnp.exp2(scores[...] - m).astype(BF16)
-        sums = nn(where_v[...], p)
-        partial[t] = jnp.concatenate([sums[0:7], m], axis=0)
-
-    corr_scores(0, scores_a, max_a)
-
-    def two_tiles(i, carry):
-        corr_scores(2 * i + 1, scores_b, max_b)
-        corr_sums(2 * i, scores_a, max_a)
-        corr_scores(jnp.minimum(2 * i + 2, GROUP - 1), scores_a, max_a)
-        corr_sums(2 * i + 1, scores_b, max_b)
-        return carry
-
-    lax.fori_loop(0, GROUP // 2, two_tiles, 0)
-
-    def hand_in(start):
+        where_v[:, CELLS * k : CELLS * (k + 1)] = weigh.astype(F32).astype(BF16)
+
+    def corr_score(u, slot):
+        def get_queries(sub):
+            t = (2 * u + sub) % 4
+            return ref_q[2 * t : 2 * t + 2].reshape(TILE, CHAN)
+
+        def get_scores(sub, j, queries):
+            return nt(ref_k[(2 * u + sub) // 4 * 4 + j], queries)
+
+        return (*held_scores[slot], get_queries, get_scores)
+
+    def corr_value(u, slot):
+        def get_values(sub, j):
+            k = (2 * u + sub) // 4 * 4 + j
+            return where_v[:, CELLS * k : CELLS * (k + 1)]
+
+        def put(sub, m, acc):
+            chunk, t = (2 * u + sub) // 4, (2 * u + sub) % 4
+            sums = jnp.concatenate([acc[0:7], m], axis=0)
+            partial[chunk, 2 * t] = sums[:, :CELLS]
+            partial[chunk, 2 * t + 1] = sums[:, CELLS:]
+
+        return (*held_scores[slot], get_values, put)
+
+    def hand_in(u, start):
+        chunk = u // 2
+
         def step(i, carry):
-            to = lax.rem(column + i, GROUP)
+            to = 4 * (u % 2) + i
             copy = pltpu.make_async_remote_copy(
-                partial.at[to], parts.at[column], part_send_sem, part_sem,
+                partial.at[chunk, to], parts.at[chunk * GROUP + column], part_send_sem, part_sem,
                 device_id=(pair, line * 8 + to, c), device_id_type=MESH,
             )
+
+            @pl.when(to != column)
+            def _():
+                if start:
+                    copy.start()
+                else:
+                    copy.wait_send()
+
             if start:
-                copy.start()
-            else:
-                copy.wait_send()
+
+                @pl.when(to == column)
+                def _():
+                    pltpu.make_async_copy(partial.at[chunk, to], parts.at[chunk * GROUP + column], part_sem).start()
+
             return carry
 
-        lax.fori_loop(1, GROUP, step, 0)
-
-    hand_in(True)
-    parts[column] = partial[column]
+        lax.fori_loop(0, 4, step, 0)
+
+    pltpu.make_async_copy(ref_q.at[0:7], ref_q.at[0:7], q_sem).wait()
+    pltpu.make_async_copy(ref_k.at[1:4], ref_k.at[1:4], k_sem).wait()
+    together(corr_score(0, 0), None)
+    together(corr_score(1, 1), corr_value(0, 0))
+    hand_in(0, True)
+    pltpu.make_async_copy(ref_k.at[4:8], ref_k.at[4:8], k_far_sem).wait()
+    together(corr_score(2, 0), corr_value(1, 1))
+    hand_in(1, True)
+    together(corr_score(3, 1), corr_value(2, 0))
+    hand_in(2, True)
+    together(None, corr_value(3, 1))
+    hand_in(3, True)
     spread("k", False)
     spread("q", False)
-    hand_in(False)
-    pltpu.make_async_copy(parts.at[0:7], parts.at[0:7], part_sem).wait()
+    for u in range(4):
+        hand_in(u, False)
+    arrived(parts, part_sem)
 
     m = jnp.max(parts[:, 7:8, :], axis=0)
-    total = jnp.zeros((8, TILE), F32)
-    for j in range(GROUP):
+    total = jnp.zeros((8, CELLS), F32)
+    for j in range(2 * GROUP):
         total = total + parts[j] * jnp.exp2(parts[j, 7:8, :] - m)
-    lane = lax.broadcasted_iota(jnp.int32, (1, TILE), 1)
+    lane = lax.broadcasted_iota(jnp.int32, (1, CELLS), 1)
     own_column = (64 * c + 32 * (lane // HALF) + lane % 32).astype(F32)
     own_row = (4 * r + (lane // 32) % 4).astype(F32)
     flows = (
@@ -371,20 +444,22 @@
 
 def shards(first, second, attend_w, merge_w, message_gain, message_bias, expand_w, reduce_w, update_gain, update_bias):
     rows = [v.reshape(1, CHAN) for v in (message_gain, message_bias, update_gain, update_bias)]
+    operands = (first, second, attend_w, merge_w, rows[0], rows[1], expand_w, reduce_w, rows[2], rows[3])
     vmem = pl.BlockSpec(memory_space=pltpu.VMEM)
     dma = pltpu.SemaphoreType.DMA
     return pl.pallas_call(
         kernel,
         out_shape=jax.ShapeDtypeStruct((2, 4, 64), F32),
-        in_specs=[vmem] * 10,
+        in_specs=[pl.BlockSpec(memory_space=pl.ANY)] * 10,
         out_specs=vmem,
-        scratch_shapes=[
+        scratch_shapes=[pltpu.VMEM(v.shape, v.dtype) for v in operands]
+        + [
             pltpu.VMEM((2, 2, HEADS, 48, HALF), BF16),
             pltpu.VMEM((CORNER, 48, HALF), BF16),
             pltpu.VMEM((EDGE, 48, HALF), BF16),
             pltpu.VMEM((OWN, 48, HALF), BF16),
             pltpu.VMEM((OTHER, 32, HALF), BF16),
-            pltpu.VMEM((16, 16, TILE), BF16),
+            pltpu.VMEM((8, 16, TILE), BF16),
             pltpu.VMEM((7 * CHUNK, 16), BF16),
             pltpu.VMEM((32, 7 * CHUNK), BF16),
             pltpu.VMEM((2 * CHUNK, TILE), F32),
@@ -395,17 +470,18 @@
             pltpu.VMEM((2 * UNITS, 8, TILE), F32),
             pltpu.VMEM((32, 16, HALF), BF16),
             pltpu.VMEM((2, 2, HEADS, 16, HALF), BF16),
-            pltpu.VMEM((GROUP, TILE, CHAN), BF16),
-            pltpu.VMEM((GROUP, TILE, CHAN), BF16),
-            pltpu.VMEM((16, GROUP * TILE), BF16),
-            pltpu.VMEM((GROUP, 8, TILE), F32),
-            pltpu.VMEM((GROUP, 8, TILE), F32),
+            pltpu.VMEM((GROUP, CELLS, CHAN), BF16),
+            pltpu.VMEM((GROUP, CELLS, CHAN), BF16),
+            pltpu.VMEM((16, GROUP * CELLS), BF16),
+            pltpu.VMEM((2, GROUP, 8, CELLS), F32),
+            pltpu.VMEM((2 * GROUP, 8, CELLS), F32),
         ]
-        + [dma] * 12,
+        + [dma] * 13
+        + [dma((10,))],
         compiler_params=pltpu.CompilerParams(
-            collective_id=0, has_side_effects=True, vmem_limit_bytes=40 * 1024 * 1024
+            collective_id=0, has_side_effects=True, vmem_limit_bytes=67000000
         ),
-    )(first, second, attend_w, merge_w, rows[0], rows[1], expand_w, reduce_w, rows[2], rows[3])
+    )(*operands)
 
 
 def solution(mesh):

time: 56.5 us -> 49.3 us (0.87)
  local copies, waits for them, and re-layouts: 6.6 us -> 1.28 us
  Pallas kernels: 49.4 us -> 47.9 us
    unnamed x21 -> x1, local copies, waits for them, and re-layouts: 6.6 us -> 1.28 us
    pallas_call x1, Pallas kernels: 49.4 us -> 47.9 us  [shards(): pl.pallas_call(kernel, out_shape=jax.ShapeDtypeStruct((2, 4, 64), F32), i...]
where the time goes in v2:
time: 49.3 us; the launch traced here: 49.1 us
  Pallas kernels  47.9 us (97%)
  local copies, waits for them, and re-layouts  1.28 us (3%)
    pallas_call x1, Pallas kernels, shards(): pl.pallas_call(kernel, out_shape=jax.ShapeDtypeStruct((2, 4, 64), F32), i...  47.9 us
    unnamed x1, local copies, waits for them, and re-layouts  1.28 us

profile of v2, /device:TPU:1, one launch (start us, length us, event | category | flops | bytes accessed | tf_op | source)
XLA Modules:
  0.0 49.1 jit_solution(3131349147812150890)
XLA Ops:
  0.0 47.9 %shard_map.100 = f32[2,4,64]{2,1,0:T(4,128)} custom-call(bf16[4,64,128]{2,1,0:T(8,128)(2,1)} %refs_0_.1, bf16[4,64,128]{2,1,0:T(8,128)(2,1)} %refs_1_.1, bf16[128,384]{1,0:T(8,128)(2,1)} %refs_2_.1, bf16[128,128]{1,0:T(8,128)(2,1)} %refs_3_.1, f32[1,128]{1,0:T(1,128)} %bitcast.4, f32[1,128]{1,0:T(1,128)} %bitcast.5, bf16[256,1024]{1,0:T(8,128)(2,1)} %refs_6_.1, ...), custom_call_target="tpu_custom_call" | custom-call | tf_op jit(solution)/shard_map/pallas_call | solution.py:450
  47.9 1.3 %copy.12 = f32[2,4,64]{2,1,0:T(4,128)} copy(f32[2,4,64]{2,1,0:T(4,128)} %shard_map.100) | data formatting | bytes 4096

commit v3 on v2

--- a/solution.py
+++ b/solution.py
@@ -25,6 +25,7 @@
 CELLS = 256
 CORNER, EDGE, OWN, OTHER = 8, 16, 8, 24
 UNITS = 9
+ORDER = (0, 1, 3, 2)
 GROUP = 8
 
 
@@ -58,28 +59,29 @@
     (
     sent, corner, edge, own, other,
     q_all, k_all, v_all, scores_a, scores_b, max_a, max_b, accs, maxes,
-    o_all, attended, ref_q, ref_k, where_v, partial, parts,
+    o_all, attended, ref_q, ref_k, where_v, running, partial, parts,
     send_sem, corner_sem, edge_sem, own_sem, other_sem,
-    back_send_sem, back_sem, ref_send_sem, q_sem, k_sem, part_send_sem, part_sem, k_far_sem, load_sem,
+    back_send_sem, back_sem, ref_send_sem, q_sem, k_sem, part_send_sem, part_sem, load_sem, core_sem,
+    relay_send_sem, relay_sem, q_pass_send_sem, q_pass_sem,
     ) = refs
     loads = [pltpu.make_async_copy(inputs[j], held[j], load_sem.at[j]) for j in range(10)]
     for j in (0, 1, 2, 3, 4, 5, 6, 7, 8, 9):
         loads[j].start()
     pair, r, c = lax.axis_index("pair"), lax.axis_index("row"), lax.axis_index("col")
-    me = r * 2 + c
-    side = r // 16
-    place = lax.rem(r, 16)
-    head, frame = place // 2, lax.rem(place, 2)
+    place, side = r >> 1, r & 1
+    head, frame = place >> 1, place & 1
+    own_side = r >> 4
     middle = (r >= 8) & (r < 24)
 
     barrier = pltpu.get_barrier_semaphore()
 
     def greet(i, carry):
-        peer = lax.rem(me + 1 + i, 64)
-        pl.semaphore_signal(barrier, inc=1, device_id=(pair, peer // 2, lax.rem(peer, 2)), device_id_type=MESH)
+        to = (r >> 1) * 2 + c + 1 + i & 31
+        pl.semaphore_signal(barrier, inc=1, device_id=(pair, (to >> 1) * 2 + (r & 1), to & 1), device_id_type=MESH)
         return carry
 
-    lax.fori_loop(0, 63, greet, 0)
+    pl.semaphore_signal(barrier, inc=1, device_id=(pair, r ^ 1, c), device_id_type=MESH)
+    lax.fori_loop(0, 31, greet, 0, unroll=True)
 
     for j in (0, 1, 2):
         loads[j].wait()
@@ -94,7 +96,9 @@
             sent[f, half, :, 16:32, :] = projected[CHAN : 2 * CHAN].astype(BF16).reshape(HEADS, 16, HALF)
             sent[f, half, :, 32:48, :] = projected[2 * CHAN :].astype(BF16).reshape(HEADS, 16, HALF)
 
-    pl.semaphore_wait(barrier, 63)
+    pl.semaphore_wait(barrier, 32)
+    pl.semaphore_signal(core_sem, inc=1, device_id=(pair, r ^ 1, c), device_id_type=MESH)
+    pl.semaphore_wait(core_sem, 1)
 
     def transfer(source, target, dest_r, dest_c, s_sem, r_sem, start):
         here = (dest_r == r) & (dest_c == c)
@@ -118,48 +122,51 @@
     def send_all(start):
         def each(body):
             def step(i, carry):
-                d = lax.rem(place + i, 16)
-                body(d // 2, lax.rem(d, 2), d)
+                d = place + i & 15
+                body(d >> 1, d & 1, d)
                 return carry
 
-            lax.fori_loop(0, 16, step, 0)
+            lax.fori_loop(0, 16, step, 0, unroll=4 if start else 1)
 
         inner = 1 - c
 
         @pl.when(middle)
         def _():
             def outer_half(h, f, d):
-                transfer(sent.at[f, c, h], edge.at[r - 8], (1 - c) * 16 + d, c, send_sem, edge_sem, start)
+                transfer(sent.at[f, c, h], edge.at[r - 8], d * 2 + 1 - c, c, send_sem, edge_sem, start)
 
             def own_half(h, f, d):
-                transfer(sent.at[f, inner, h], own.at[lax.rem(r, 8)], side * 16 + d, c, send_sem, own_sem, start)
-
-            def other_halves(h, f, d):
-                for turn in range(1, 4):
-                    to_side, to_c = side ^ (turn // 2), c ^ (turn % 2)
-                    transfer(
-                        sent.at[f, inner, h, 16:48],
-                        other.at[(turn - 1) * 8 + lax.rem(r, 8)],
-                        to_side * 16 + d, to_c, send_sem, other_sem, start,
-                    )
+                transfer(sent.at[f, inner, h], own.at[r & 7], d * 2 + own_side, c, send_sem, own_sem, start)
+
+            def other_half(h, f, d):
+                transfer(
+                    sent.at[f, inner, h, 16:48], other.at[r & 7], d * 2 + own_side, 1 - c, send_sem, other_sem, start
+                )
 
             each(outer_half)
             each(own_half)
-            each(other_halves)
+            each(other_half)
 
         @pl.when(jnp.logical_not(middle))
         def _():
             def corner_half(h, f, d):
-                transfer(sent.at[f, c, h], corner.at[lax.rem(r, 8)], side * 16 + d, c, send_sem, corner_sem, start)
+                transfer(sent.at[f, c, h], corner.at[r & 7], d * 2 + own_side, c, send_sem, corner_sem, start)
 
             def edge_half(h, f, d):
-                slot = c * 8 + lax.rem(r, 8)
-                transfer(sent.at[f, inner, h], edge.at[slot], side * 16 + d, side, send_sem, edge_sem, start)
+                slot = c * 8 + (r & 7)
+                transfer(sent.at[f, inner, h], edge.at[slot], d * 2 + own_side, own_side, send_sem, edge_sem, start)
 
             each(corner_half)
             each(edge_half)
 
     send_all(True)
+
+    relays = [
+        pltpu.make_async_remote_copy(
+            source, target, relay_send_sem, relay_sem, device_id=(pair, r ^ 1, c), device_id_type=MESH
+        )
+        for source, target in ((own.at[:, 16:48], other.at[8:16]), (other.at[0:8], other.at[16:24]))
+    ]
 
     def arrived(ref, sem):
         pltpu.make_async_copy(ref, ref, sem).wait()
@@ -171,8 +178,8 @@
     def take_q(block, at):
         q_all[at // 4, :, (at % 4) * HALF : (at % 4 + 1) * HALF] = block[0:16, :]
 
-    def together(score, value):
-        for sub in range(2):
+    def together(score, value, tiles=2, chunk=CHUNK):
+        for sub in range(tiles):
             if score:
                 scores, top, get_queries, get_keys = score
                 queries = get_queries(sub)
@@ -181,8 +188,8 @@
                 lifted, tops, get_values, put = value
                 m = jnp.max(tops[sub], axis=0, keepdims=True)
                 acc = None
-            for j in range(CHUNK // PIECE):
-                at = slice(sub * CHUNK + j * PIECE, sub * CHUNK + (j + 1) * PIECE)
+            for j in range(chunk // PIECE):
+                at = slice(sub * chunk + j * PIECE, sub * chunk + (j + 1) * PIECE)
                 if score:
                     x = get_keys(sub, j, queries)
                     scores[at, :] = x
@@ -241,35 +248,44 @@
         for b in range(4):
             o_all[4 * tile + b] = o[:, b * HALF : (b + 1) * HALF]
 
-    def give_back(kind, start):
+    def give_back(kind, start, first=0, count=8):
         def step(j, carry):
+            j = j + first
             if kind == "corner":
                 at, to_r, to_c, half = j, side * 24 + j, c, c
             elif kind == "edge":
                 level = side == c
                 at = CORNER + j
-                to_r = jnp.where(level, side * 24 + lax.rem(j, 8), 8 + j)
-                to_c = jnp.where(level, j // 8, c)
+                to_r = jnp.where(level, side * 24 + (j & 7), 8 + j)
+                to_c = jnp.where(level, j >> 3, c)
                 half = jnp.where(level, 1 - to_c, to_c)
             else:
                 at, to_r, to_c, half = CORNER + EDGE + j, 8 + 8 * side + j, c, 1 - c
             transfer(o_all.at[at], attended.at[frame, half, head], to_r, to_c, back_send_sem, back_sem, start)
             return carry
 
-        lax.fori_loop(0, EDGE if kind == "edge" else 8, step, 0)
+        lax.fori_loop(0, count, step, 0, unroll=True if start else 1)
 
     def two_units(i, carry):
         @pl.when(i == 2)
         def _():
+            for b in range(8):
+                take_kv(other[b], 32 + b, 0)
+            arrived(other.at[8:24], relay_sem)
+            for b in range(8, OTHER):
+                take_kv(other[b], 32 + b, 0)
+
+        together(attend_score(2 * i + 1, 1), attend_value(2 * i, 0))
+
+        @pl.when(i == 1)
+        def _():
             arrived(own, own_sem)
+            arrived(other.at[0:8], other_sem)
+            for copy in relays:
+                copy.start()
             for b in range(OWN):
                 take_kv(own[b], 24 + b, 16)
                 take_q(own[b], 24 + b)
-            arrived(other, other_sem)
-            for b in range(OTHER):
-                take_kv(other[b], 32 + b, 0)
-
-        together(attend_score(2 * i + 1, 1), attend_value(2 * i, 0))
 
         @pl.when(i == 2)
         def _():
@@ -278,20 +294,17 @@
             give_back("corner", True)
             for tile in range(4):
                 finish(2 + tile, 2 + 2 * tile, 2)
-            give_back("edge", True)
+            give_back("edge", True, 0, 16)
 
         together(attend_score(2 * i + 2, 0), attend_value(2 * i + 1, 1))
         return carry
 
     lax.fori_loop(0, UNITS // 2, two_units, 0)
+    finish(6, 10, 4)
+    give_back("centre", True, 0, 4)
     together(None, attend_value(UNITS - 1, 0))
-    for tile in range(2):
-        finish(6 + tile, 10 + 4 * tile, 4)
-    give_back("centre", True)
-
-    send_all(False)
-    for kind in ("corner", "edge", "centre"):
-        give_back(kind, False)
+    finish(7, 14, 4)
+    give_back("centre", True, 4, 4)
     arrived(attended, back_sem)
     for j in range(3, 10):
         loads[j].wait()
@@ -311,122 +324,134 @@
             update = update + nn(hidden, reduce_w[256 * j : 256 * j + 256, :])
         return cells.astype(F32) + layer_norm(update, update_gain[...], update_bias[...])
 
-    column, line = lax.rem(r, 8), r // 8
+    column, line = r & 7, r >> 3
 
     def spread(kind, start):
         def step(i, carry):
             if kind == "k":
-                to_line, to_c = lax.rem(line + i // 2, 4), c ^ lax.rem(i, 2)
-                at = lax.rem(4 - i // 2, 4) * 2 + lax.rem(i, 2)
-                for near in (True, False):
-
-                    @pl.when((at < 4) == near)
-                    def _():
-                        copy = pltpu.make_async_remote_copy(
-                            ref_k.at[0], ref_k.at[at], ref_send_sem, k_sem if near else k_far_sem,
-                            device_id=(pair, to_line * 8 + column, to_c), device_id_type=MESH,
-                        )
-                        if start:
-                            copy.start()
-                        else:
-                            copy.wait_send()
+                to_line, to_c = line + (i >> 1) & 3, c ^ (i & 1)
+                at = (4 - (i >> 1) & 3) * 2 + (i & 1)
+                ref, sem, to_r = ref_k, k_sem.at[at >> 1], to_line * 8 + column
             else:
-                copy = pltpu.make_async_remote_copy(
-                    ref_q.at[column], ref_q.at[column], ref_send_sem, q_sem,
-                    device_id=(pair, line * 8 + lax.rem(column + i, GROUP), c), device_id_type=MESH,
-                )
-                if start:
-                    copy.start()
-                else:
-                    copy.wait_send()
+                to_c, at = c, (4 - (i >> 1) & 3) * 2 + (i & 1)
+                ref, sem, to_r = ref_q, q_pass_sem.at[0] if i == 1 else q_sem.at[at >> 1], line * 8 + ((column >> 1) + (i >> 1) & 3) * 2 + (column & 1 ^ i & 1)
+            copy = pltpu.make_async_remote_copy(
+                ref.at[0], ref.at[at], ref_send_sem, sem, device_id=(pair, to_r, to_c), device_id_type=MESH
+            )
+            if start:
+                copy.start()
+            else:
+                copy.wait_send()
             return carry
 
-        lax.fori_loop(1, GROUP, step, 0)
+        if start:
+            for i in (1, 2, 3, 6, 7, 4, 5) if kind == "k" else (1, 2, 6, 4):
+                step(i, 0)
+        else:
+            for i in range(1, GROUP) if kind == "k" else (1, 2, 6, 4):
+                step(i, 0)
 
     ref_k[0] = refine(1, second).astype(BF16)
     spread("k", True)
-    ref_q[column] = (refine(0, first) * (LOG2E / math.sqrt(CHAN))).astype(BF16)
+    ref_q[0] = (refine(0, first) * (LOG2E / math.sqrt(CHAN))).astype(BF16)
     spread("q", True)
 
     at = lax.broadcasted_iota(jnp.int32, (16, CELLS), 1)
     what = lax.broadcasted_iota(jnp.int32, (16, CELLS), 0)
     for k in range(GROUP):
         key_column = 64 * (c ^ (k % 2)) + 32 * (at // HALF) + at % 32
-        key_row = 4 * (8 * lax.rem(line + k // 2, 4) + column) + (at // 32) % 4
+        key_row = 4 * (8 * (line + k // 2 & 3) + column) + (at // 32) % 4
         weigh = jnp.where(what == 0, 1, jnp.where(what == 1, key_column, key_row))
         where_v[:, CELLS * k : CELLS * (k + 1)] = weigh.astype(F32).astype(BF16)
 
     def corr_score(u, slot):
         def get_queries(sub):
-            t = (2 * u + sub) % 4
+            t = ORDER[sub]
+            if u == 0:
+                arrived(ref_q.at[2 * t + 1], q_pass_sem.at[t])
             return ref_q[2 * t : 2 * t + 2].reshape(TILE, CHAN)
 
         def get_scores(sub, j, queries):
-            return nt(ref_k[(2 * u + sub) // 4 * 4 + j], queries)
+            return nt(ref_k[2 * ORDER[u] + j], queries)
 
         return (*held_scores[slot], get_queries, get_scores)
 
     def corr_value(u, slot):
         def get_values(sub, j):
-            k = (2 * u + sub) // 4 * 4 + j
+            k = 2 * ORDER[u] + j
             return where_v[:, CELLS * k : CELLS * (k + 1)]
 
         def put(sub, m, acc):
-            chunk, t = (2 * u + sub) // 4, (2 * u + sub) % 4
-            sums = jnp.concatenate([acc[0:7], m], axis=0)
-            partial[chunk, 2 * t] = sums[:, :CELLS]
-            partial[chunk, 2 * t + 1] = sums[:, CELLS:]
+            sums = acc[0:8]
+            if u:
+                before, m_before = running[sub, 0:8], running[sub, 8:9]
+                m_now = jnp.maximum(m, m_before)
+                sums = sums * jnp.exp2(m - m_now) + before * jnp.exp2(m_before - m_now)
+                m = m_now
+            if u < 3:
+                running[sub, 0:8] = sums
+                running[sub, 8:16] = jnp.broadcast_to(m, (8, TILE))
+            else:
+                sums = jnp.concatenate([sums[0:7], m], axis=0)
+                partial[2 * sub] = sums[:, :CELLS]
+                partial[2 * sub + 1] = sums[:, CELLS:]
+                hand_in(sub, True)
 
         return (*held_scores[slot], get_values, put)
 
-    def hand_in(u, start):
-        chunk = u // 2
-
-        def step(i, carry):
-            to = 4 * (u % 2) + i
+    def hand_in(sub, start):
+        for i in range(2):
+            at = 2 * ORDER[sub] + i
+            if at == 0:
+                if start:
+                    parts[0] = partial[0]
+                continue
+            to = ((column >> 1) + ORDER[sub] & 3) * 2 + (column & 1 ^ i)
             copy = pltpu.make_async_remote_copy(
-                partial.at[chunk, to], parts.at[chunk * GROUP + column], part_send_sem, part_sem,
+                partial.at[2 * sub + i], parts.at[(4 - ORDER[sub]) % 4 * 2 + i], part_send_sem, part_sem,
                 device_id=(pair, line * 8 + to, c), device_id_type=MESH,
             )
-
-            @pl.when(to != column)
-            def _():
-                if start:
-                    copy.start()
-                else:
-                    copy.wait_send()
-
             if start:
-
-                @pl.when(to == column)
-                def _():
-                    pltpu.make_async_copy(partial.at[chunk, to], parts.at[chunk * GROUP + column], part_sem).start()
-
-            return carry
-
-        lax.fori_loop(0, 4, step, 0)
-
-    pltpu.make_async_copy(ref_q.at[0:7], ref_q.at[0:7], q_sem).wait()
-    pltpu.make_async_copy(ref_k.at[1:4], ref_k.at[1:4], k_sem).wait()
-    together(corr_score(0, 0), None)
-    together(corr_score(1, 1), corr_value(0, 0))
-    hand_in(0, True)
-    pltpu.make_async_copy(ref_k.at[4:8], ref_k.at[4:8], k_far_sem).wait()
-    together(corr_score(2, 0), corr_value(1, 1))
-    hand_in(1, True)
-    together(corr_score(3, 1), corr_value(2, 0))
-    hand_in(2, True)
-    together(None, corr_value(3, 1))
-    hand_in(3, True)
+                copy.start()
+            else:
+                copy.wait_send()
+
+    passes = []
+    for t in ORDER[1:]:
+        arrived(ref_q.at[2 * t], q_sem.at[t])
+        copy = pltpu.make_async_remote_copy(
+            ref_q.at[2 * t], ref_q.at[2 * t + 1], q_pass_send_sem, q_pass_sem.at[t],
+            device_id=(pair, r ^ 1, c), device_id_type=MESH,
+        )
+        copy.start()
+        passes.append(copy)
+
+    def corr(score, value):
+        together(score, value, tiles=4, chunk=2 * CELLS)
+
+    arrived(ref_k.at[1:2], k_sem.at[0])
+    corr(corr_score(0, 0), None)
+    for u in range(1, 4):
+        arrived(ref_k.at[2 * ORDER[u] : 2 * ORDER[u] + 2], k_sem.at[ORDER[u]])
+        corr(corr_score(u, u % 2), corr_value(u - 1, (u - 1) % 2))
+    corr(None, corr_value(3, 1))
+    for copy in relays:
+        copy.wait_send()
+    send_all(False)
+    give_back("corner", False)
+    give_back("edge", False, 0, 16)
+    give_back("centre", False)
     spread("k", False)
     spread("q", False)
-    for u in range(4):
-        hand_in(u, False)
-    arrived(parts, part_sem)
+    for copy in passes:
+        copy.wait_send()
+    for sub in range(4):
+        hand_in(sub, False)
+    arrived(parts.at[1:8], part_sem)
 
     m = jnp.max(parts[:, 7:8, :], axis=0)
     total = jnp.zeros((8, CELLS), F32)
-    for j in range(2 * GROUP):
+    for j in range(GROUP):
         total = total + parts[j] * jnp.exp2(parts[j, 7:8, :] - m)
     lane = lax.broadcasted_iota(jnp.int32, (1, CELLS), 1)
     own_column = (64 * c + 32 * (lane // HALF) + lane % 32).astype(F32)
@@ -464,8 +489,8 @@
             pltpu.VMEM((32, 7 * CHUNK), BF16),
             pltpu.VMEM((2 * CHUNK, TILE), F32),
             pltpu.VMEM((2 * CHUNK, TILE), F32),
-            pltpu.VMEM((2, 8, TILE), F32),
-            pltpu.VMEM((2, 8, TILE), F32),
+            pltpu.VMEM((4, 8, TILE), F32),
+            pltpu.VMEM((4, 8, TILE), F32),
             pltpu.VMEM((2 * UNITS, 32, TILE), F32),
             pltpu.VMEM((2 * UNITS, 8, TILE), F32),
             pltpu.VMEM((32, 16, HALF), BF16),
@@ -473,11 +498,12 @@
             pltpu.VMEM((GROUP, CELLS, CHAN), BF16),
             pltpu.VMEM((GROUP, CELLS, CHAN), BF16),
             pltpu.VMEM((16, GROUP * CELLS), BF16),
-            pltpu.VMEM((2, GROUP, 8, CELLS), F32),
-            pltpu.VMEM((2 * GROUP, 8, CELLS), F32),
+            pltpu.VMEM((4, 16, TILE), F32),
+            pltpu.VMEM((GROUP, 8, CELLS), F32),
+            pltpu.VMEM((GROUP, 8, CELLS), F32),
         ]
-        + [dma] * 13
-        + [dma((10,))],
+        + [dma] * 8
+        + [dma((4,)), dma((4,)), dma, dma, dma((10,)), pltpu.SemaphoreType.REGULAR, dma, dma, dma, dma((4,))],
         compiler_params=pltpu.CompilerParams(
             collective_id=0, has_side_effects=True, vmem_limit_bytes=67000000
         ),

time: 49.3 us -> 47.7 us (0.968); the launches traced: 49.1 us -> 46.7 us
  Pallas kernels: 47.9 us -> 45.4 us
    pallas_call x1, Pallas kernels: 47.9 us -> 45.4 us  [shards(): pl.pallas_call(kernel, out_shape=jax.ShapeDtypeStruct((2, 4, 64), F32), i...]
where the time goes in v3:
time: 47.7 us; the launch traced here: 46.7 us
  Pallas kernels  45.4 us (95%)
  local copies, waits for them, and re-layouts  1.28 us (3%)
    pallas_call x1, Pallas kernels, shards(): pl.pallas_call(kernel, out_shape=jax.ShapeDtypeStruct((2, 4, 64), F32), i...  45.4 us
    unnamed x1, local copies, waits for them, and re-layouts  1.28 us

profile of v3, /device:TPU:1, one launch (start us, length us, event | category | flops | bytes accessed | tf_op | source)
XLA Modules:
  0.0 46.7 jit_solution(16423523708499809932)
XLA Ops:
  0.0 45.4 %shard_map.100 = f32[2,4,64]{2,1,0:T(4,128)} custom-call(bf16[4,64,128]{2,1,0:T(8,128)(2,1)} %refs_0_.1, bf16[4,64,128]{2,1,0:T(8,128)(2,1)} %refs_1_.1, bf16[128,384]{1,0:T(8,128)(2,1)} %refs_2_.1, bf16[128,128]{1,0:T(8,128)(2,1)} %refs_3_.1, f32[1,128]{1,0:T(1,128)} %bitcast.4, f32[1,128]{1,0:T(1,128)} %bitcast.5, bf16[256,1024]{1,0:T(8,128)(2,1)} %refs_6_.1, ...), custom_call_target="tpu_custom_call" | custom-call | tf_op jit(solution)/shard_map/pallas_call | solution.py:475
  45.4 1.3 %copy.12 = f32[2,4,64]{2,1,0:T(4,128)} copy(f32[2,4,64]{2,1,0:T(4,128)} %shard_map.100) | data formatting | bytes 4096

commit v4 on v3

--- a/solution.py
+++ b/solution.py
@@ -252,16 +252,17 @@
         def step(j, carry):
             j = j + first
             if kind == "corner":
-                at, to_r, to_c, half = j, side * 24 + j, c, c
+                at, to_r, to_c, late = j, side * 24 + j, c, 0
             elif kind == "edge":
                 level = side == c
                 at = CORNER + j
                 to_r = jnp.where(level, side * 24 + (j & 7), 8 + j)
                 to_c = jnp.where(level, j >> 3, c)
-                half = jnp.where(level, 1 - to_c, to_c)
+                late = jnp.where(level, 1, 0)
             else:
-                at, to_r, to_c, half = CORNER + EDGE + j, 8 + 8 * side + j, c, 1 - c
-            transfer(o_all.at[at], attended.at[frame, half, head], to_r, to_c, back_send_sem, back_sem, start)
+                at, to_r, to_c, late = CORNER + EDGE + j, 8 + 8 * side + j, c, 1
+            target = attended.at[late, frame, head]
+            transfer(o_all.at[at], target, to_r, to_c, back_send_sem, back_sem.at[late], start)
             return carry
 
         lax.fori_loop(0, count, step, 0, unroll=True if start else 1)
@@ -305,16 +306,14 @@
     together(None, attend_value(UNITS - 1, 0))
     finish(7, 14, 4)
     give_back("centre", True, 4, 4)
-    arrived(attended, back_sem)
     for j in range(3, 10):
         loads[j].wait()
 
-    def refine(f, source):
-        cells = jnp.concatenate(
-            [source[:, 32 * half : 32 * half + 32, :].reshape(HALF, CHAN) for half in range(2)], axis=0
-        )
+    def refine(late):
+        local = pl.ds(pl.multiple_of(32 * (1 - c if late else c), 32), 32)
+        cells = jnp.concatenate([source[:, local, :].reshape(HALF, CHAN) for source in (second, first)], axis=0)
         heads = jnp.concatenate(
-            [attended[f, half].reshape(CHAN, HALF).astype(F32).T.astype(BF16) for half in range(2)], axis=0
+            [attended[late, f].reshape(CHAN, HALF).astype(F32).T.astype(BF16) for f in (1, 0)], axis=0
         )
         message = layer_norm(nn(heads, merge_w[...]), message_gain[...], message_bias[...]).astype(BF16)
         joined = jnp.concatenate([cells, message], axis=1)
@@ -322,11 +321,15 @@
         for j in range(HIDDEN // 256):
             hidden = erf_gelu(nn(joined, expand_w[:, 256 * j : 256 * j + 256])).astype(BF16)
             update = update + nn(hidden, reduce_w[256 * j : 256 * j + 256, :])
-        return cells.astype(F32) + layer_norm(update, update_gain[...], update_bias[...])
+        refined = cells.astype(F32) + layer_norm(update, update_gain[...], update_bias[...])
+        ref_k[0, late * HALF : (late + 1) * HALF, :] = refined[:HALF].astype(BF16)
+        ref_q[0, late * HALF : (late + 1) * HALF, :] = (refined[HALF:] * (LOG2E / math.sqrt(CHAN))).astype(BF16)
 
     column, line = r & 7, r >> 3
 
-    def spread(kind, start):
+    def spread(kind, late, start):
+        half = pl.ds(late * HALF, HALF)
+
         def step(i, carry):
             if kind == "k":
                 to_line, to_c = line + (i >> 1) & 3, c ^ (i & 1)
@@ -336,7 +339,7 @@
                 to_c, at = c, (4 - (i >> 1) & 3) * 2 + (i & 1)
                 ref, sem, to_r = ref_q, q_pass_sem.at[0] if i == 1 else q_sem.at[at >> 1], line * 8 + ((column >> 1) + (i >> 1) & 3) * 2 + (column & 1 ^ i & 1)
             copy = pltpu.make_async_remote_copy(
-                ref.at[0], ref.at[at], ref_send_sem, sem, device_id=(pair, to_r, to_c), device_id_type=MESH
+                ref.at[0, half], ref.at[at, half], ref_send_sem, sem, device_id=(pair, to_r, to_c), device_id_type=MESH
             )
             if start:
                 copy.start()
@@ -351,15 +354,17 @@
             for i in range(1, GROUP) if kind == "k" else (1, 2, 6, 4):
                 step(i, 0)
 
-    ref_k[0] = refine(1, second).astype(BF16)
-    spread("k", True)
-    ref_q[0] = (refine(0, first) * (LOG2E / math.sqrt(CHAN))).astype(BF16)
-    spread("q", True)
+    for late in range(2):
+        arrived(attended.at[late], back_sem.at[late])
+        refine(late)
+        spread("k", late, True)
+        spread("q", late, True)
 
     at = lax.broadcasted_iota(jnp.int32, (16, CELLS), 1)
     what = lax.broadcasted_iota(jnp.int32, (16, CELLS), 0)
     for k in range(GROUP):
-        key_column = 64 * (c ^ (k % 2)) + 32 * (at // HALF) + at % 32
+        key_c = c ^ (k % 2)
+        key_column = 64 * key_c + 32 * jnp.where(at < HALF, key_c, 1 - key_c) + at % 32
         key_row = 4 * (8 * (line + k // 2 & 3) + column) + (at // 32) % 4
         weigh = jnp.where(what == 0, 1, jnp.where(what == 1, key_column, key_row))
         where_v[:, CELLS * k : CELLS * (k + 1)] = weigh.astype(F32).astype(BF16)
@@ -441,8 +446,9 @@
     give_back("corner", False)
     give_back("edge", False, 0, 16)
     give_back("centre", False)
-    spread("k", False)
-    spread("q", False)
+    for late in range(2):
+        spread("k", late, False)
+        spread("q", late, False)
     for copy in passes:
         copy.wait_send()
     for sub in range(4):
@@ -454,7 +460,7 @@
     for j in range(GROUP):
         total = total + parts[j] * jnp.exp2(parts[j, 7:8, :] - m)
     lane = lax.broadcasted_iota(jnp.int32, (1, CELLS), 1)
-    own_column = (64 * c + 32 * (lane // HALF) + lane % 32).astype(F32)
+    own_column = (64 * c + 32 * jnp.where(lane < HALF, c, 1 - c) + lane % 32).astype(F32)
     own_row = (4 * r + (lane // 32) % 4).astype(F32)
     flows = (
         (total[1:2] / total[0:1] - own_column) * (2.0 / 128),
@@ -462,9 +468,9 @@
     )
     for which in range(2):
         for i in range(4):
-            for half in range(2):
-                start = half * HALF + 32 * i
-                out[which, i : i + 1, 32 * half : 32 * half + 32] = flows[which][:, start : start + 32]
+            early, late = (flows[which][:, at : at + 32] for at in (32 * i, HALF + 32 * i))
+            out[which, i : i + 1, 0:32] = jnp.where(c == 0, early, late)
+            out[which, i : i + 1, 32:64] = jnp.where(c == 0, late, early)
 
 
 def shards(first, second, attend_w, merge_w, message_gain, message_bias, expand_w, reduce_w, update_gain, update_bias):
@@ -502,7 +508,8 @@
             pltpu.VMEM((GROUP, 8, CELLS), F32),
             pltpu.VMEM((GROUP, 8, CELLS), F32),
         ]
-        + [dma] * 8
+        + [dma] * 6
+        + [dma((2,)), dma]
         + [dma((4,)), dma((4,)), dma, dma, dma((10,)), pltpu.SemaphoreType.REGULAR, dma, dma, dma, dma((4,))],
         compiler_params=pltpu.CompilerParams(
             collective_id=0, has_side_effects=True, vmem_limit_bytes=67000000

time: 47.7 us -> 45.1 us (0.945); the launches traced: 46.7 us -> 45 us
  Pallas kernels: 45.4 us -> 43.7 us
    pallas_call x1, Pallas kernels: 45.4 us -> 43.7 us  [shards(): pl.pallas_call(kernel, out_shape=jax.ShapeDtypeStruct((2, 4, 64), F32), i...]
where the time goes in v4:
time: 45.1 us; the launch traced here: 45 us
  Pallas kernels  43.7 us (97%)
  local copies, waits for them, and re-layouts  1.28 us (3%)
    pallas_call x1, Pallas kernels, shards(): pl.pallas_call(kernel, out_shape=jax.ShapeDtypeStruct((2, 4, 64), F32), i...  43.7 us
    unnamed x1, local copies, waits for them, and re-layouts  1.28 us

profile of v4, /device:TPU:1, one launch (start us, length us, event | category | flops | bytes accessed | tf_op | source)
XLA Modules:
  0.0 45.0 jit_solution(16079630535886512311)
XLA Ops:
  0.0 43.7 %shard_map.100 = f32[2,4,64]{2,1,0:T(4,128)} custom-call(bf16[4,64,128]{2,1,0:T(8,128)(2,1)} %refs_0_.1, bf16[4,64,128]{2,1,0:T(8,128)(2,1)} %refs_1_.1, bf16[128,384]{1,0:T(8,128)(2,1)} %refs_2_.1, bf16[128,128]{1,0:T(8,128)(2,1)} %refs_3_.1, f32[1,128]{1,0:T(1,128)} %bitcast.4, f32[1,128]{1,0:T(1,128)} %bitcast.5, bf16[256,1024]{1,0:T(8,128)(2,1)} %refs_6_.1, ...), custom_call_target="tpu_custom_call" | custom-call | tf_op jit(solution)/shard_map/pallas_call | solution.py:481
  43.7 1.3 %copy.12 = f32[2,4,64]{2,1,0:T(4,128)} copy(f32[2,4,64]{2,1,0:T(4,128)} %shard_map.100) | data formatting | bytes 4096

commit v5 on v4

--- a/solution.py
+++ b/solution.py
@@ -22,7 +22,6 @@
 TILE = 512
 CHUNK = 1024
 PIECE = 256
-CELLS = 256
 CORNER, EDGE, OWN, OTHER = 8, 16, 8, 24
 UNITS = 9
 ORDER = (0, 1, 3, 2)
@@ -322,24 +321,22 @@
             hidden = erf_gelu(nn(joined, expand_w[:, 256 * j : 256 * j + 256])).astype(BF16)
             update = update + nn(hidden, reduce_w[256 * j : 256 * j + 256, :])
         refined = cells.astype(F32) + layer_norm(update, update_gain[...], update_bias[...])
-        ref_k[0, late * HALF : (late + 1) * HALF, :] = refined[:HALF].astype(BF16)
-        ref_q[0, late * HALF : (late + 1) * HALF, :] = (refined[HALF:] * (LOG2E / math.sqrt(CHAN))).astype(BF16)
+        ref_k[late, 0] = refined[:HALF].astype(BF16)
+        ref_q[late, 0] = (refined[HALF:] * (LOG2E / math.sqrt(CHAN))).astype(BF16)
 
     column, line = r & 7, r >> 3
 
     def spread(kind, late, start):
-        half = pl.ds(late * HALF, HALF)
-
         def step(i, carry):
             if kind == "k":
                 to_line, to_c = line + (i >> 1) & 3, c ^ (i & 1)
                 at = (4 - (i >> 1) & 3) * 2 + (i & 1)
-                ref, sem, to_r = ref_k, k_sem.at[at >> 1], to_line * 8 + column
+                ref, sem, to_r = ref_k, k_sem.at[late], to_line * 8 + column
             else:
                 to_c, at = c, (4 - (i >> 1) & 3) * 2 + (i & 1)
-                ref, sem, to_r = ref_q, q_pass_sem.at[0] if i == 1 else q_sem.at[at >> 1], line * 8 + ((column >> 1) + (i >> 1) & 3) * 2 + (column & 1 ^ i & 1)
+                ref, sem, to_r = ref_q, q_pass_sem.at[late] if i == 1 else q_sem.at[4 * late + (at >> 1)], line * 8 + ((column >> 1) + (i >> 1) & 3) * 2 + (column & 1 ^ i & 1)
             copy = pltpu.make_async_remote_copy(
-                ref.at[0, half], ref.at[at, half], ref_send_sem, sem, device_id=(pair, to_r, to_c), device_id_type=MESH
+                ref.at[late, 0], ref.at[late, at], ref_send_sem, sem, device_id=(pair, to_r, to_c), device_id_type=MESH
             )
             if start:
                 copy.start()
@@ -360,60 +357,55 @@
         spread("k", late, True)
         spread("q", late, True)
 
-    at = lax.broadcasted_iota(jnp.int32, (16, CELLS), 1)
-    what = lax.broadcasted_iota(jnp.int32, (16, CELLS), 0)
-    for k in range(GROUP):
-        key_c = c ^ (k % 2)
-        key_column = 64 * key_c + 32 * jnp.where(at < HALF, key_c, 1 - key_c) + at % 32
-        key_row = 4 * (8 * (line + k // 2 & 3) + column) + (at // 32) % 4
-        weigh = jnp.where(what == 0, 1, jnp.where(what == 1, key_column, key_row))
-        where_v[:, CELLS * k : CELLS * (k + 1)] = weigh.astype(F32).astype(BF16)
-
-    def corr_score(u, slot):
+    at = lax.broadcasted_iota(jnp.int32, (16, HALF), 1)
+    what = lax.broadcasted_iota(jnp.int32, (16, HALF), 0)
+    for late in range(2):
+        for k in range(GROUP):
+            key_c = c ^ (k % 2)
+            key_column = 64 * key_c + 32 * (1 - key_c if late else key_c) + at % 32
+            key_row = 4 * (8 * (line + k // 2 & 3) + column) + at // 32
+            weigh = jnp.where(what == 0, 1, jnp.where(what == 1, key_column, key_row))
+            where_v[late, :, HALF * k : HALF * (k + 1)] = weigh.astype(F32).astype(BF16)
+
+    def corr_score(late_k, late_q, slot):
         def get_queries(sub):
-            t = ORDER[sub]
-            if u == 0:
-                arrived(ref_q.at[2 * t + 1], q_pass_sem.at[t])
-            return ref_q[2 * t : 2 * t + 2].reshape(TILE, CHAN)
+            return ref_q[late_q, 4 * sub : 4 * sub + 4].reshape(TILE, CHAN)
 
         def get_scores(sub, j, queries):
-            return nt(ref_k[2 * ORDER[u] + j], queries)
+            return nt(ref_k[late_k, 2 * j : 2 * j + 2].reshape(PIECE, CHAN), queries)
 
         return (*held_scores[slot], get_queries, get_scores)
 
-    def corr_value(u, slot):
+    def corr_value(late_k, late_q, slot):
         def get_values(sub, j):
-            k = 2 * ORDER[u] + j
-            return where_v[:, CELLS * k : CELLS * (k + 1)]
+            return where_v[late_k, :, PIECE * j : PIECE * (j + 1)]
 
         def put(sub, m, acc):
-            sums = acc[0:8]
-            if u:
-                before, m_before = running[sub, 0:8], running[sub, 8:9]
-                m_now = jnp.maximum(m, m_before)
-                sums = sums * jnp.exp2(m - m_now) + before * jnp.exp2(m_before - m_now)
-                m = m_now
-            if u < 3:
-                running[sub, 0:8] = sums
-                running[sub, 8:16] = jnp.broadcast_to(m, (8, TILE))
-            else:
-                sums = jnp.concatenate([sums[0:7], m], axis=0)
-                partial[2 * sub] = sums[:, :CELLS]
-                partial[2 * sub + 1] = sums[:, CELLS:]
-                hand_in(sub, True)
+            sums, at = acc[0:8], 2 * late_q + sub
+            if not late_k:
+                running[at, 0:8] = sums
+                running[at, 8:16] = jnp.broadcast_to(m, (8, TILE))
+                return
+            before, m_before = running[at, 0:8], running[at, 8:9]
+            m_now = jnp.maximum(m, m_before)
+            sums = sums * jnp.exp2(m - m_now) + before * jnp.exp2(m_before - m_now)
+            sums = jnp.concatenate([sums[0:7], m_now], axis=0)
+            for j in range(4):
+                partial[late_q, 4 * sub + j] = sums[:, HALF * j : HALF * (j + 1)]
+            hand_in(late_q, sub, True)
 
         return (*held_scores[slot], get_values, put)
 
-    def hand_in(sub, start):
-        for i in range(2):
-            at = 2 * ORDER[sub] + i
+    def hand_in(late, sub, start):
+        for at in range(4 * sub, 4 * sub + 4):
+            t, i = at // 2, at % 2
             if at == 0:
                 if start:
-                    parts[0] = partial[0]
+                    parts[late, 0] = partial[late, 0]
                 continue
-            to = ((column >> 1) + ORDER[sub] & 3) * 2 + (column & 1 ^ i)
+            to = ((column >> 1) + t & 3) * 2 + (column & 1 ^ i)
             copy = pltpu.make_async_remote_copy(
-                partial.at[2 * sub + i], parts.at[(4 - ORDER[sub]) % 4 * 2 + i], part_send_sem, part_sem,
+                partial.at[late, at], parts.at[late, (4 - t) % 4 * 2 + i], part_send_sem, part_sem.at[late],
                 device_id=(pair, line * 8 + to, c), device_id_type=MESH,
             )
             if start:
@@ -422,53 +414,62 @@
                 copy.wait_send()
 
     passes = []
-    for t in ORDER[1:]:
-        arrived(ref_q.at[2 * t], q_sem.at[t])
-        copy = pltpu.make_async_remote_copy(
-            ref_q.at[2 * t], ref_q.at[2 * t + 1], q_pass_send_sem, q_pass_sem.at[t],
-            device_id=(pair, r ^ 1, c), device_id_type=MESH,
-        )
-        copy.start()
-        passes.append(copy)
-
-    def corr(score, value):
-        together(score, value, tiles=4, chunk=2 * CELLS)
-
-    arrived(ref_k.at[1:2], k_sem.at[0])
-    corr(corr_score(0, 0), None)
-    for u in range(1, 4):
-        arrived(ref_k.at[2 * ORDER[u] : 2 * ORDER[u] + 2], k_sem.at[ORDER[u]])
-        corr(corr_score(u, u % 2), corr_value(u - 1, (u - 1) % 2))
-    corr(None, corr_value(3, 1))
+
+    def pass_on(late):
+        for t in ORDER[1:]:
+            arrived(ref_q.at[late, 2 * t], q_sem.at[4 * late + t])
+            copy = pltpu.make_async_remote_copy(
+                ref_q.at[late, 2 * t], ref_q.at[late, 2 * t + 1], q_pass_send_sem, q_pass_sem.at[late],
+                device_id=(pair, r ^ 1, c), device_id_type=MESH,
+            )
+            copy.start()
+            passes.append(copy)
+
+    pass_on(0)
+    arrived(ref_k.at[0, 1:8], k_sem.at[0])
+    arrived(ref_q.at[0, 0:4], q_pass_sem.at[0])
+    together(corr_score(0, 0, 0), None)
+    together(None, corr_value(0, 0, 0))
+    pass_on(1)
+    arrived(ref_q.at[1, 0:4], q_pass_sem.at[1])
+    together(corr_score(0, 1, 1), None)
+    arrived(ref_k.at[1, 1:8], k_sem.at[1])
+    together(corr_score(1, 0, 0), corr_value(0, 1, 1))
+    together(corr_score(1, 1, 1), corr_value(1, 0, 0))
+    together(None, corr_value(1, 1, 1))
     for copy in relays:
         copy.wait_send()
     send_all(False)
     give_back("corner", False)
     give_back("edge", False, 0, 16)
     give_back("centre", False)
+    for copy in passes:
+        copy.wait_send()
     for late in range(2):
         spread("k", late, False)
         spread("q", late, False)
-    for copy in passes:
-        copy.wait_send()
-    for sub in range(4):
-        hand_in(sub, False)
-    arrived(parts.at[1:8], part_sem)
-
-    m = jnp.max(parts[:, 7:8, :], axis=0)
-    total = jnp.zeros((8, CELLS), F32)
-    for j in range(GROUP):
-        total = total + parts[j] * jnp.exp2(parts[j, 7:8, :] - m)
-    lane = lax.broadcasted_iota(jnp.int32, (1, CELLS), 1)
-    own_column = (64 * c + 32 * jnp.where(lane < HALF, c, 1 - c) + lane % 32).astype(F32)
-    own_row = (4 * r + (lane // 32) % 4).astype(F32)
-    flows = (
-        (total[1:2] / total[0:1] - own_column) * (2.0 / 128),
-        (total[2:3] / total[0:1] - own_row) * (2.0 / 128),
-    )
+        hand_in(late, 0, False)
+        hand_in(late, 1, False)
+
+    lane = lax.broadcasted_iota(jnp.int32, (1, HALF), 1)
+    flows = []
+    for late in range(2):
+        arrived(parts.at[late, 1:8], part_sem.at[late])
+        m = jnp.max(parts[late, :, 7:8, :], axis=0)
+        total = jnp.zeros((8, HALF), F32)
+        for j in range(GROUP):
+            total = total + parts[late, j] * jnp.exp2(parts[late, j, 7:8, :] - m)
+        own_column = (64 * c + 32 * (1 - c if late else c) + lane % 32).astype(F32)
+        own_row = (4 * r + lane // 32).astype(F32)
+        flows.append(
+            (
+                (total[1:2] / total[0:1] - own_column) * (2.0 / 128),
+                (total[2:3] / total[0:1] - own_row) * (2.0 / 128),
+            )
+        )
     for which in range(2):
         for i in range(4):
-            early, late = (flows[which][:, at : at + 32] for at in (32 * i, HALF + 32 * i))
+            early, late = (flow[which][:, 32 * i : 32 * i + 32] for flow in flows)
             out[which, i : i + 1, 0:32] = jnp.where(c == 0, early, late)
             out[which, i : i + 1, 32:64] = jnp.where(c == 0, late, early)
 
@@ -501,16 +502,16 @@
             pltpu.VMEM((2 * UNITS, 8, TILE), F32),
             pltpu.VMEM((32, 16, HALF), BF16),
             pltpu.VMEM((2, 2, HEADS, 16, HALF), BF16),
-            pltpu.VMEM((GROUP, CELLS, CHAN), BF16),
-            pltpu.VMEM((GROUP, CELLS, CHAN), BF16),
-            pltpu.VMEM((16, GROUP * CELLS), BF16),
+            pltpu.VMEM((2, GROUP, HALF, CHAN), BF16),
+            pltpu.VMEM((2, GROUP, HALF, CHAN), BF16),
+            pltpu.VMEM((2, 16, GROUP * HALF), BF16),
             pltpu.VMEM((4, 16, TILE), F32),
-            pltpu.VMEM((GROUP, 8, CELLS), F32),
-            pltpu.VMEM((GROUP, 8, CELLS), F32),
+            pltpu.VMEM((2, GROUP, 8, HALF), F32),
+            pltpu.VMEM((2, GROUP, 8, HALF), F32),
         ]
         + [dma] * 6
         + [dma((2,)), dma]
-        + [dma((4,)), dma((4,)), dma, dma, dma((10,)), pltpu.SemaphoreType.REGULAR, dma, dma, dma, dma((4,))],
+        + [dma((8,)), dma((2,)), dma, dma((2,)), dma((10,)), pltpu.SemaphoreType.REGULAR, dma, dma, dma, dma((2,))],
         compiler_params=pltpu.CompilerParams(
             collective_id=0, has_side_effects=True, vmem_limit_bytes=67000000
         ),

time: 45.1 us -> 44.9 us (level)
  no operation moved by 1% of the time
where the time goes in v5:
time: 44.9 us; the launch traced here: 44.8 us
  Pallas kernels  43.5 us (97%)
  local copies, waits for them, and re-layouts  1.28 us (3%)
    pallas_call x1, Pallas kernels, shards(): pl.pallas_call(kernel, out_shape=jax.ShapeDtypeStruct((2, 4, 64), F32), i...  43.5 us
    unnamed x1, local copies, waits for them, and re-layouts  1.28 us

profile of v5, /device:TPU:1, one launch (start us, length us, event | category | flops | bytes accessed | tf_op | source)
XLA Modules:
  0.0 44.8 jit_solution(8479613084085073762)
XLA Ops:
  0.0 43.5 %shard_map.100 = f32[2,4,64]{2,1,0:T(4,128)} custom-call(bf16[4,64,128]{2,1,0:T(8,128)(2,1)} %refs_0_.1, bf16[4,64,128]{2,1,0:T(8,128)(2,1)} %refs_1_.1, bf16[128,384]{1,0:T(8,128)(2,1)} %refs_2_.1, bf16[128,128]{1,0:T(8,128)(2,1)} %refs_3_.1, f32[1,128]{1,0:T(1,128)} %bitcast.4, f32[1,128]{1,0:T(1,128)} %bitcast.5, bf16[256,1024]{1,0:T(8,128)(2,1)} %refs_6_.1, ...), custom_call_target="tpu_custom_call" | custom-call | tf_op jit(solution)/shard_map/pallas_call | solution.py:482
  43.5 1.3 %copy.12 = f32[2,4,64]{2,1,0:T(4,128)} copy(f32[2,4,64]{2,1,0:T(4,128)} %shard_map.100) | data formatting | bytes 4096

commit v6 on v5

--- a/solution.py
+++ b/solution.py
@@ -26,6 +26,10 @@
 UNITS = 9
 ORDER = (0, 1, 3, 2)
 GROUP = 8
+
+
+HOPS = (0, 1, 2, 1)
+OFFSETS = sorted(((dx, dy) for dx in range(4) for dy in range(4)), key=lambda d: -HOPS[d[0]] - HOPS[d[1]])
 
 
 def nn(a, b):
@@ -74,13 +78,11 @@
 
     barrier = pltpu.get_barrier_semaphore()
 
-    def greet(i, carry):
-        to = (r >> 1) * 2 + c + 1 + i & 31
-        pl.semaphore_signal(barrier, inc=1, device_id=(pair, (to >> 1) * 2 + (r & 1), to & 1), device_id_type=MESH)
-        return carry
-
+    for dx, dy in OFFSETS:
+        to = ((r >> 3) + dx & 3) * 8 + ((r >> 1) + dy & 3) * 2 + (r & 1)
+        for to_c in (1 - c, c) if dx or dy else (1 - c,):
+            pl.semaphore_signal(barrier, inc=1, device_id=(pair, to, to_c), device_id_type=MESH)
     pl.semaphore_signal(barrier, inc=1, device_id=(pair, r ^ 1, c), device_id_type=MESH)
-    lax.fori_loop(0, 31, greet, 0, unroll=True)
 
     for j in (0, 1, 2):
         loads[j].wait()
@@ -99,7 +101,17 @@
     pl.semaphore_signal(core_sem, inc=1, device_id=(pair, r ^ 1, c), device_id_type=MESH)
     pl.semaphore_wait(core_sem, 1)
 
-    def transfer(source, target, dest_r, dest_c, s_sem, r_sem, start):
+    def transfer(source, target, dest_r, dest_c, s_sem, r_sem, start, near):
+        if not near:
+            copy = pltpu.make_async_remote_copy(
+                source, target, s_sem, r_sem, device_id=(pair, dest_r, dest_c), device_id_type=MESH
+            )
+            if start:
+                copy.start()
+            else:
+                copy.wait_send()
+            return
+
         here = (dest_r == r) & (dest_c == c)
 
         @pl.when(jnp.logical_not(here))
@@ -120,26 +132,23 @@
 
     def send_all(start):
         def each(body):
-            def step(i, carry):
-                d = place + i & 15
-                body(d >> 1, d & 1, d)
-                return carry
-
-            lax.fori_loop(0, 16, step, 0, unroll=4 if start else 1)
+            for dx, dy in OFFSETS:
+                d = ((r >> 3) + dx & 3) * 4 + ((r >> 1) + dy & 3)
+                body(d >> 1, d & 1, d, not (dx or dy))
 
         inner = 1 - c
 
         @pl.when(middle)
         def _():
-            def outer_half(h, f, d):
-                transfer(sent.at[f, c, h], edge.at[r - 8], d * 2 + 1 - c, c, send_sem, edge_sem, start)
-
-            def own_half(h, f, d):
-                transfer(sent.at[f, inner, h], own.at[r & 7], d * 2 + own_side, c, send_sem, own_sem, start)
-
-            def other_half(h, f, d):
+            def outer_half(h, f, d, near):
+                transfer(sent.at[f, c, h], edge.at[r - 8], d * 2 + 1 - c, c, send_sem, edge_sem, start, near)
+
+            def own_half(h, f, d, near):
+                transfer(sent.at[f, inner, h], own.at[r & 7], d * 2 + own_side, c, send_sem, own_sem, start, near)
+
+            def other_half(h, f, d, near):
                 transfer(
-                    sent.at[f, inner, h, 16:48], other.at[r & 7], d * 2 + own_side, 1 - c, send_sem, other_sem, start
+                    sent.at[f, inner, h, 16:48], other.at[r & 7], d * 2 + own_side, 1 - c, send_sem, other_sem, start, False
                 )
 
             each(outer_half)
@@ -148,12 +157,12 @@
 
         @pl.when(jnp.logical_not(middle))
         def _():
-            def corner_half(h, f, d):
-                transfer(sent.at[f, c, h], corner.at[r & 7], d * 2 + own_side, c, send_sem, corner_sem, start)
-
-            def edge_half(h, f, d):
+            def corner_half(h, f, d, near):
+                transfer(sent.at[f, c, h], corner.at[r & 7], d * 2 + own_side, c, send_sem, corner_sem, start, near)
+
+            def edge_half(h, f, d, near):
                 slot = c * 8 + (r & 7)
-                transfer(sent.at[f, inner, h], edge.at[slot], d * 2 + own_side, own_side, send_sem, edge_sem, start)
+                transfer(sent.at[f, inner, h], edge.at[slot], d * 2 + own_side, own_side, send_sem, edge_sem, start, near)
 
             each(corner_half)
             each(edge_half)
@@ -261,7 +270,7 @@
             else:
                 at, to_r, to_c, late = CORNER + EDGE + j, 8 + 8 * side + j, c, 1
             target = attended.at[late, frame, head]
-            transfer(o_all.at[at], target, to_r, to_c, back_send_sem, back_sem.at[late], start)
+            transfer(o_all.at[at], target, to_r, to_c, back_send_sem, back_sem.at[late], start, True)
             return carry
 
         lax.fori_loop(0, count, step, 0, unroll=True if start else 1)
@@ -354,8 +363,8 @@
     for late in range(2):
         arrived(attended.at[late], back_sem.at[late])
         refine(late)
+        spread("q", late, True)
         spread("k", late, True)
-        spread("q", late, True)
 
     at = lax.broadcasted_iota(jnp.int32, (16, HALF), 1)
     what = lax.broadcasted_iota(jnp.int32, (16, HALF), 0)
@@ -429,8 +438,8 @@
     arrived(ref_k.at[0, 1:8], k_sem.at[0])
     arrived(ref_q.at[0, 0:4], q_pass_sem.at[0])
     together(corr_score(0, 0, 0), None)
+    pass_on(1)
     together(None, corr_value(0, 0, 0))
-    pass_on(1)
     arrived(ref_q.at[1, 0:4], q_pass_sem.at[1])
     together(corr_score(0, 1, 1), None)
     arrived(ref_k.at[1, 1:8], k_sem.at[1])
@@ -513,7 +522,7 @@
         + [dma((2,)), dma]
         + [dma((8,)), dma((2,)), dma, dma((2,)), dma((10,)), pltpu.SemaphoreType.REGULAR, dma, dma, dma, dma((2,))],
         compiler_params=pltpu.CompilerParams(
-            collective_id=0, has_side_effects=True, vmem_limit_bytes=67000000
+            collective_id=0, has_side_effects=True, vmem_limit_bytes=56522000
         ),
     )(*operands)
 

time: 44.9 us -> 44.1 us (0.982)
  Pallas kernels: 43.5 us -> 42.7 us
    pallas_call x1, Pallas kernels: 43.5 us -> 42.7 us  [shards(): pl.pallas_call(kernel, out_shape=jax.ShapeDtypeStruct((2, 4, 64), F32), i...]
    unnamed x1 -> x9, local copies, waits for them, and re-layouts: 1.28 us -> 1.28 us
where the time goes in v6:
time: 44.1 us; the launch traced here: 44 us
  Pallas kernels  42.7 us (97%)
  local copies, waits for them, and re-layouts  1.28 us (3%)
    pallas_call x1, Pallas kernels, shards(): pl.pallas_call(kernel, out_shape=jax.ShapeDtypeStruct((2, 4, 64), F32), i...  42.7 us
    unnamed x9, local copies, waits for them, and re-layouts  1.28 us

profile of v6, /device:TPU:1, one launch (start us, length us, event | category | flops | bytes accessed | tf_op | source)
XLA Modules:
  0.0 44.0 jit_solution(7473065865125097110)
XLA Ops:
  0.0 0.0 copy-start.3
  0.0 0.0 copy-start
  0.0 0.0 copy-start.1
  0.0 0.0 copy-start.2
  0.0 0.6 %copy-done.3 = f32[128]{0:T(128)S(1)} copy-done((f32[128]{0:T(128)S(1)}, f32[128]{0:T(128)}, u32[]{:S(2)}) %copy-start.3) | copy-done | bytes 536
  0.7 0.0 copy-done
  0.7 0.0 copy-done.1
  0.7 0.0 copy-done.2
  0.7 42.7 %shard_map.100 = f32[2,4,64]{2,1,0:T(4,128)S(1)} custom-call(bf16[4,64,128]{2,1,0:T(8,128)(2,1)} %refs_0_.1, bf16[4,64,128]{2,1,0:T(8,128)(2,1)} %refs_1_.1, bf16[128,384]{1,0:T(8,128)(2,1)} %refs_2_.1, bf16[128,128]{1,0:T(8,128)(2,1)} %refs_3_.1, f32[1,128]{1,0:T(1,128)S(1)} %bitcast.4, f32[1,128]{1,0:T(1,128)S(1)} %bitcast.5, bf16[256,1024]{1,0:T(8,128)(2,1)} %refs_6_.1, ...), custom_call_target="tpu_custom_call" | custom-call | tf_op jit(solution)/shard_map/pallas_call | solution.py:491
  43.4 0.6 %copy.12 = f32[2,4,64]{2,1,0:T(4,128)} copy(f32[2,4,64]{2,1,0:T(4,128)S(1)} %shard_map.100) | data formatting | bytes 4096
Async XLA Ops:
  0.0 0.7 %copy-start.3 = (f32[128]{0:T(128)S(1)}, f32[128]{0:T(128)}, u32[]{:S(2)}) copy-start(f32[128]{0:T(128)} %param.19) | copy-start | bytes 1540
  0.0 0.7 %copy-start = (f32[128]{0:T(128)S(1)}, f32[128]{0:T(128)}, u32[]{:S(2)}) copy-start(f32[128]{0:T(128)} %param.14) | copy-start | bytes 1540
  0.0 0.7 %copy-start.1 = (f32[128]{0:T(128)S(1)}, f32[128]{0:T(128)}, u32[]{:S(2)}) copy-start(f32[128]{0:T(128)} %param.15) | copy-start | bytes 1540
  0.0 0.7 %copy-start.2 = (f32[128]{0:T(128)S(1)}, f32[128]{0:T(128)}, u32[]{:S(2)}) copy-start(f32[128]{0:T(128)} %param.18) | copy-start | bytes 1540

commit v7 on v6

--- a/solution.py
+++ b/solution.py
@@ -68,7 +68,7 @@
     relay_send_sem, relay_sem, q_pass_send_sem, q_pass_sem,
     ) = refs
     loads = [pltpu.make_async_copy(inputs[j], held[j], load_sem.at[j]) for j in range(10)]
-    for j in (0, 1, 2, 3, 4, 5, 6, 7, 8, 9):
+    for j in (0, 1, 2):
         loads[j].start()
     pair, r, c = lax.axis_index("pair"), lax.axis_index("row"), lax.axis_index("col")
     place, side = r >> 1, r & 1
@@ -84,6 +84,8 @@
             pl.semaphore_signal(barrier, inc=1, device_id=(pair, to, to_c), device_id_type=MESH)
     pl.semaphore_signal(barrier, inc=1, device_id=(pair, r ^ 1, c), device_id_type=MESH)
 
+    for j in range(3, 10):
+        loads[j].start()
     for j in (0, 1, 2):
         loads[j].wait()
 

time: 44.1 us -> 44.1 us (level)
  no operation moved by 1% of the time
where the time goes in v7:
time: 44.1 us; the launch traced here: 44 us
  Pallas kernels  42.7 us (97%)
  local copies, waits for them, and re-layouts  1.28 us (3%)
    pallas_call x1, Pallas kernels, shards(): pl.pallas_call(kernel, out_shape=jax.ShapeDtypeStruct((2, 4, 64), F32), i...  42.7 us
    unnamed x9, local copies, waits for them, and re-layouts  1.28 us

profile of v7, /device:TPU:1, one launch (start us, length us, event | category | flops | bytes accessed | tf_op | source)
XLA Modules:
  0.0 44.0 jit_solution(10120976628191605997)
XLA Ops:
  0.0 0.0 copy-start.3
  0.0 0.0 copy-start
  0.0 0.0 copy-start.1
  0.0 0.0 copy-start.2
  0.0 0.6 %copy-done.3 = f32[128]{0:T(128)S(1)} copy-done((f32[128]{0:T(128)S(1)}, f32[128]{0:T(128)}, u32[]{:S(2)}) %copy-start.3) | copy-done | bytes 536
  0.7 0.0 copy-done
  0.7 0.0 copy-done.1
  0.7 0.0 copy-done.2
  0.7 42.7 %shard_map.100 = f32[2,4,64]{2,1,0:T(4,128)S(1)} custom-call(bf16[4,64,128]{2,1,0:T(8,128)(2,1)} %refs_0_.1, bf16[4,64,128]{2,1,0:T(8,128)(2,1)} %refs_1_.1, bf16[128,384]{1,0:T(8,128)(2,1)} %refs_2_.1, bf16[128,128]{1,0:T(8,128)(2,1)} %refs_3_.1, f32[1,128]{1,0:T(1,128)S(1)} %bitcast.4, f32[1,128]{1,0:T(1,128)S(1)} %bitcast.5, bf16[256,1024]{1,0:T(8,128)(2,1)} %refs_6_.1, ...), custom_call_target="tpu_custom_call" | custom-call | tf_op jit(solution)/shard_map/pallas_call | solution.py:493
  43.4 0.6 %copy.12 = f32[2,4,64]{2,1,0:T(4,128)} copy(f32[2,4,64]{2,1,0:T(4,128)S(1)} %shard_map.100) | data formatting | bytes 4096
Async XLA Ops:
  0.0 0.7 %copy-start.3 = (f32[128]{0:T(128)S(1)}, f32[128]{0:T(128)}, u32[]{:S(2)}) copy-start(f32[128]{0:T(128)} %param.19) | copy-start | bytes 1540
  0.0 0.7 %copy-start = (f32[128]{0:T(128)S(1)}, f32[128]{0:T(128)}, u32[]{:S(2)}) copy-start(f32[128]{0:T(128)} %param.14) | copy-start | bytes 1540
  0.0 0.7 %copy-start.1 = (f32[128]{0:T(128)S(1)}, f32[128]{0:T(128)}, u32[]{:S(2)}) copy-start(f32[128]{0:T(128)} %param.15) | copy-start | bytes 1540
  0.0 0.7 %copy-start.2 = (f32[128]{0:T(128)S(1)}, f32[128]{0:T(128)}, u32[]{:S(2)}) copy-start(f32[128]{0:T(128)} %param.18) | copy-start | bytes 1540
